TPU v7x, 256 devices: a whole 4x4x8 slice. The times are simulated.
256 devices in a mesh: dp: 32 (over x, z), seq: 8 (over y, core).
Axes of the slice: x: 4, y: 4, z: 8, core: 2. Of those that a mesh axis runs over, the one named last changes fastest.
Arguments:
- normed_block_input: bfloat16 [32, 1024, 8192], P('dp', 'seq'), may hold values from -6 to 6
- saved_queries: bfloat16 [32, 1024, 4096], P('dp', 'seq'), may hold values from -40 to 40
- saved_keys: bfloat16 [32, 1024, 512], P('dp', 'seq'), may hold values from -6 to 6
- saved_values: bfloat16 [32, 1024, 512], P('dp', 'seq'), may hold values from -6 to 6
- attention_output: bfloat16 [32, 1024, 4096], P('dp', 'seq'), may hold values from -6 to 6
- output_gradient: bfloat16 [32, 1024, 4096], P('dp', 'seq'), may hold values from -6 to 6
- adapter_down_weight: bfloat16 [8192, 192], replicated, may hold values from -0.0625 to 0.0625
- query_up_weight: bfloat16 [64, 4096], replicated, may hold values from -0.75 to 0.75
- key_up_weight: bfloat16 [64, 512], replicated, may hold values from -0.75 to 0.75
- value_up_weight: bfloat16 [64, 512], replicated, may hold values from -0.75 to 0.75
Outputs:
- query_gradient: bfloat16 [32, 1024, 4096], P('dp', 'seq')
- key_gradient: bfloat16 [32, 1024, 512], P('dp', 'seq')
- value_gradient: bfloat16 [32, 1024, 512], P('dp', 'seq')
- down_grad: float32 [8192, 192], P(('dp', 'seq'))
- up_grad_q: float32 [64, 4096], replicated
- up_grad_k: float32 [64, 512], replicated
- up_grad_v: float32 [64, 512], replicated
All inputs are finite; a program needn't handle non-finite values.
Results may differ from a plain program's by a relative error of at most 0.0065.
Values may be sent and summed in bfloat16 or wider, within the bound.
A program may use at most 128 MiB of HBM per device.

v0:
```python
import math

import jax
import jax.numpy as jnp
from jax import lax
from jax.sharding import PartitionSpec as P

HEAD_SIZE = 128


ADAPTER_SCALE = 0.25


def contract_rows(left, right):
    return lax.dot_general(
        left, right, (((0,), (0,)), ((), ())), preferred_element_type=jnp.float32
    )


def contract_columns(left, right):
    return lax.dot_general(
        left, right, (((1,), (1,)), ((), ())), preferred_element_type=jnp.float32
    )


def attention_back(queries, keys_dev, values_dev, grads, deltas):
    span_length, kv_local, group_size, head_dim = queries.shape
    block = min(512, span_length)
    score_scale = head_dim ** (-0.5)
    key_pos = jnp.arange(span_length)

    def one_block(running, block_index):
        key_acc, value_acc = running
        first_row = block_index * block
        query_blk = lax.dynamic_slice_in_dim(queries, first_row, block, 0)
        grad_blk = lax.dynamic_slice_in_dim(grads, first_row, block, 0)
        delta_blk = lax.dynamic_slice_in_dim(deltas, first_row, block, 0)
        scores = (
            jnp.einsum("qkgd,skd->kgqs", query_blk, keys_dev, preferred_element_type=jnp.float32)
            * score_scale
        )
        query_pos = first_row + jnp.arange(block)
        visible = key_pos[None, :] <= query_pos[:, None]
        scores = jnp.where(visible, scores, -jnp.inf)
        row_max = jnp.max(scores, axis=-1, keepdims=True)
        weights = jnp.exp(scores - row_max)
        probability = weights / jnp.sum(weights, axis=-1, keepdims=True)
        probs_low = probability.astype(jnp.bfloat16)
        value_acc = value_acc + jnp.einsum(
            "kgqs,qkgd->skd", probs_low, grad_blk, preferred_element_type=jnp.float32
        )
        prob_grad = jnp.einsum(
            "qkgd,skd->kgqs", grad_blk, values_dev, preferred_element_type=jnp.float32
        )
        score_grad = probability * (prob_grad - jnp.transpose(delta_blk, (1, 2, 0))[..., None])
        score_low = score_grad.astype(jnp.bfloat16)
        block_grad = (
            jnp.einsum("kgqs,skd->qkgd", score_low, keys_dev, preferred_element_type=jnp.float32)
            * score_scale
        )
        key_acc = key_acc + jnp.einsum(
            "kgqs,qkgd->skd", score_low, query_blk, preferred_element_type=jnp.float32
        )
        return ((key_acc, value_acc), block_grad.astype(jnp.bfloat16))

    empty = jnp.zeros((span_length, kv_local, head_dim), jnp.float32)
    totals, query_blocks = lax.scan(one_block, (empty, empty), jnp.arange(span_length // block))
    query_gradient = query_blocks.reshape(span_length, kv_local * group_size * head_dim)
    key_gradient = (
        (totals[0] * score_scale).astype(jnp.bfloat16).reshape(span_length, kv_local * head_dim)
    )
    value_gradient = totals[1].astype(jnp.bfloat16).reshape(span_length, kv_local * head_dim)
    return (query_gradient, key_gradient, value_gradient)


def body(
    normed_block_input,
    saved_queries,
    saved_keys,
    saved_values,
    attention_output,
    output_gradient,
    adapter_down_weight,
    query_up_weight,
    key_up_weight,
    value_up_weight,
):
    sequence_count = lax.axis_size("seq")
    slabs_total, token_rows, q_width = saved_queries.shape
    kv_width = saved_keys.shape[2]
    head_dim = HEAD_SIZE
    q_heads = q_width // head_dim
    kv_heads = kv_width // head_dim
    repeat_factor = max(1, sequence_count // kv_heads)
    kv_local = kv_heads * repeat_factor // sequence_count
    q_local = q_heads // sequence_count
    group_size = q_local // kv_local
    span_length = token_rows * sequence_count

    def to_heads(array_in):
        return array_in.reshape(
            slabs_total, token_rows, sequence_count, array_in.shape[2] // sequence_count
        )

    def widen(array_in):
        widened = jnp.broadcast_to(
            array_in.reshape(slabs_total, token_rows, kv_heads, 1, head_dim),
            (slabs_total, token_rows, kv_heads, repeat_factor, head_dim),
        )
        return widened.reshape(slabs_total, token_rows, kv_heads * repeat_factor * head_dim)

    query_in, key_in, value_in, grad_in, output_in = (
        lax.all_to_all(to_heads(saved_queries), "seq", split_axis=2, concat_axis=1, tiled=True),
        lax.all_to_all(to_heads(widen(saved_keys)), "seq", split_axis=2, concat_axis=1, tiled=True),
        lax.all_to_all(
            to_heads(widen(saved_values)), "seq", split_axis=2, concat_axis=1, tiled=True
        ),
        lax.all_to_all(to_heads(output_gradient), "seq", split_axis=2, concat_axis=1, tiled=True),
        lax.all_to_all(to_heads(attention_output), "seq", split_axis=2, concat_axis=1, tiled=True),
    )
    grad_wide = grad_in.reshape(slabs_total, span_length, q_local, head_dim).astype(jnp.float32)
    output_wide = output_in.reshape(slabs_total, span_length, q_local, head_dim).astype(jnp.float32)
    deltas = jnp.sum(grad_wide * output_wide, axis=-1)
    deltas = deltas.reshape(slabs_total, span_length, kv_local, group_size)
    queries = query_in.reshape(slabs_total, span_length, kv_local, group_size, head_dim)
    grads = grad_in.reshape(slabs_total, span_length, kv_local, group_size, head_dim)
    query_heads, key_heads, value_heads = jax.vmap(attention_back)(
        queries, key_in, value_in, grads, deltas
    )
    query_back, key_back, value_back = (
        lax.all_to_all(
            query_heads.reshape(slabs_total, span_length, 1, q_local * head_dim),
            "seq",
            split_axis=1,
            concat_axis=2,
            tiled=True,
        ),
        lax.all_to_all(
            key_heads.reshape(slabs_total, span_length, 1, kv_local * head_dim),
            "seq",
            split_axis=1,
            concat_axis=2,
            tiled=True,
        ),
        lax.all_to_all(
            value_heads.reshape(slabs_total, span_length, 1, kv_local * head_dim),
            "seq",
            split_axis=1,
            concat_axis=2,
            tiled=True,
        ),
    )
    query_gradient = query_back.reshape(slabs_total, token_rows, q_heads * head_dim)
    key_gradient = jnp.sum(
        key_back.reshape(slabs_total, token_rows, kv_heads, repeat_factor, head_dim).astype(
            jnp.float32
        ),
        axis=3,
    )
    key_gradient = key_gradient.astype(jnp.bfloat16).reshape(
        slabs_total, token_rows, kv_heads * head_dim
    )
    value_gradient = jnp.sum(
        value_back.reshape(slabs_total, token_rows, kv_heads, repeat_factor, head_dim).astype(
            jnp.float32
        ),
        axis=3,
    )
    value_gradient = value_gradient.astype(jnp.bfloat16).reshape(
        slabs_total, token_rows, kv_heads * head_dim
    )
    low_rank_size = query_up_weight.shape[0]
    flattened_input = normed_block_input.reshape(
        slabs_total * token_rows, normed_block_input.shape[2]
    )
    flattened_queries = query_gradient.reshape(slabs_total * token_rows, q_heads * head_dim)
    flattened_keys = key_gradient.reshape(slabs_total * token_rows, kv_heads * head_dim)
    flattened_values = value_gradient.reshape(slabs_total * token_rows, kv_heads * head_dim)
    down_activation = jnp.dot(
        flattened_input, adapter_down_weight, preferred_element_type=jnp.float32
    ).astype(jnp.bfloat16)
    multiplier = ADAPTER_SCALE / math.sqrt(
        slabs_total * token_rows * sequence_count * lax.axis_size("dp")
    )
    up_term_q = multiplier * contract_rows(down_activation[:, :low_rank_size], flattened_queries)
    up_term_k = multiplier * contract_rows(
        down_activation[:, low_rank_size : 2 * low_rank_size], flattened_keys
    )
    up_term_v = multiplier * contract_rows(
        down_activation[:, 2 * low_rank_size :], flattened_values
    )
    middle_term = jnp.concatenate(
        [
            contract_columns(flattened_queries, query_up_weight),
            contract_columns(flattened_keys, key_up_weight),
            contract_columns(flattened_values, value_up_weight),
        ],
        axis=1,
    ).astype(jnp.bfloat16)
    shard_rows = flattened_input.shape[1] // lax.axis_size(("dp", "seq"))
    down_term = multiplier * contract_rows(flattened_input, middle_term)
    down_total, up_grad_q, up_grad_k, up_grad_v = lax.psum(
        (down_term, up_term_q, up_term_k, up_term_v), ("dp", "seq")
    )
    down_grad = lax.dynamic_slice_in_dim(
        down_total, lax.axis_index(("dp", "seq")) * shard_rows, shard_rows, 0
    )
    return (
        query_gradient,
        key_gradient,
        value_gradient,
        down_grad,
        up_grad_q,
        up_grad_k,
        up_grad_v,
    )


def solution(mesh):
    return jax.shard_map(
        body,
        mesh=mesh,
        in_specs=(
            P("dp", "seq", None),
            P("dp", "seq", None),
            P("dp", "seq", None),
            P("dp", "seq", None),
            P("dp", "seq", None),
            P("dp", "seq", None),
            P(),
            P(),
            P(),
            P(),
        ),
        out_specs=(
            P("dp", "seq", None),
            P("dp", "seq", None),
            P("dp", "seq", None),
            P(("dp", "seq"), None),
            P(),
            P(),
            P(),
        ),
        check_vma=False,
    )
```

profile of v0, /device:TPU:1, one launch (start us, length us, event | category | flops | bytes accessed | tf_op | source)
XLA Modules:
  0.0 518.8 jit_solution(209266343198400087)
XLA Ops:
  7.2 1.1 broadcast_in_dim.44
  9.0 6.6 %all-to-all-start.1 = ((bf16[1,128,8,128]{3,1,0,2:T(8,128)(2,1)}), bf16[1,128,8,128]{3,1,0,2:T(8,128)(2,1)S(1)}, u32[]{:S(2)}, u32[]{:S(2)}) async-start(bf16[1,128,8,128]{3,1,0,2:T(8,128)(2,1)} %bitcast.283), calls=%async_computation.1 | async-start | bytes 524288 | tf_op jit(solution)/shard_map/all_to_all | solution.py:114
  15.6 2.3 copy.103
  17.9 4.2 all-to-all-done.1
  22.1 5.2 all-to-all-start
  27.3 2.3 copy.106
  29.5 13.0 %all-to-all-done = bf16[1,128,8,512]{1,3,0,2:T(8,128)(2,1)} async-done(((bf16[1,128,8,512]{1,3,0,2:T(8,128)(2,1)}), bf16[1,128,8,512]{1,3,0,2:T(8,128)(2,1)}, u32[]{:S(2)}, u32[]{:S(2)}) %all-to-all-start) | async-done | bytes 1048608 | tf_op jit(solution)/shard_map/all_to_all | solution.py:113
  42.5 5.0 all-to-all-start.2
  47.5 2.3 copy.109
  49.8 12.9 %all-to-all-done.2 = bf16[1,128,8,512]{1,3,0,2:T(8,128)(2,1)} async-done(((bf16[1,128,8,512]{1,3,0,2:T(8,128)(2,1)}), bf16[1,128,8,512]{1,3,0,2:T(8,128)(2,1)}, u32[]{:S(2)}, u32[]{:S(2)}) %all-to-all-start.2) | async-done | bytes 1048608 | tf_op jit(solution)/shard_map/all_to_all | solution.py:118
  62.7 5.0 all-to-all-start.4
  69.3 2.9 copy.104
  72.2 2.3 reshape.169
  74.5 2.9 copy.107
  77.4 2.3 reshape.171
  79.7 3.3 all-to-all-done.4
  83.7 4.8 all-to-all-start.3
  88.5 1.7 fusion.40
  90.2 2.6 copy.111
  92.8 2.7 mul.79
  95.5 1.8 reduce_sum.42
  97.3 40.1 %while.18 = (s32[]{:T(128)}, f32[1,1024,1,128]{1,3,2,0:T(8,128)}, f32[1,1024,1,128]{1,3,2,0:T(8,128)}, bf16[2,1,512,1,4,128]{5,4,2,0,3,1:T(4,128)(2,1)}, s32[2]{...) while((s32[]{:T(128)}, f32[1,1024,1,128]{1,3,2,0:T(8,128)}, ...), condition=%wide.region_4.5_spmd.clone, body=%wide.region_1.4_spmd.clone.sunk | while | flops 2725769728 | bytes 80566264 | solution.py:67
  99.1 3.3 fusion.90
  102.5 2.4 fusion.91
  104.9 3.0 fusion.94
  108.0 5.7 %fusion.92 = bf16[4,512,1024]{2,1,0:T(8,128)(2,1)S(1)} fusion(f32[4,512]{1,0:T(4,128)S(1)} %dynamic-slice_bitcast_fusion.2, f32[4,512]{1,0:T(4,128)S(1)} %fusion.91, f32[4,512]{1,0:T(4,128)S(1)} %get-tuple-element.319, f32[512,4,1024]{2,0,1:T(8,128)S(1)} %get-tuple-element.318, pred[512,1024]{1,0:T(8,128)(4,1)S(1)} %iota_compare_fusion.2, ...), kind=kOutput, calls=%fused_computation.9.clone.1 | convolution fusion | flops 551550976 | bytes 13918720 | tf_op jit(solution)/shard_map/vmap()/while/body/eval_jaxpr/qkgd,skd->kgqs/dot_general | solution.py:52
  114.6 1.3 fusion.95
  119.2 3.3 fusion.90
  122.5 2.4 fusion.91
  124.9 3.0 fusion.94
  128.0 5.7 %fusion.92 = bf16[4,512,1024]{2,1,0:T(8,128)(2,1)S(1)} fusion(f32[4,512]{1,0:T(4,128)S(1)} %dynamic-slice_bitcast_fusion.2, f32[4,512]{1,0:T(4,128)S(1)} %fusion.91, f32[4,512]{1,0:T(4,128)S(1)} %get-tuple-element.319, f32[512,4,1024]{2,0,1:T(8,128)S(1)} %get-tuple-element.318, pred[512,1024]{1,0:T(8,128)(4,1)S(1)} %iota_compare_fusion.2, ...), kind=kOutput, calls=%fused_computation.9.clone.1 | convolution fusion | flops 551550976 | bytes 13918720 | tf_op jit(solution)/shard_map/vmap()/while/body/eval_jaxpr/qkgd,skd->kgqs/dot_general | solution.py:52
  134.7 1.3 fusion.95
  137.4 1.1 convert_element_type.75
  138.5 1.1 copy.121
  140.1 3.1 reduce.10
  144.0 4.8 all-to-all-start.7
  148.8 2.0 copy.117
  150.8 1.1 multiply_convert_fusion
  151.9 1.2 copy.148
  153.1 3.8 reduce.9
  156.9 1.7 reshape.291
  158.7 4.8 all-to-all-start.6
  163.5 3.2 fusion.44
  166.6 6.9 %transpose.72 = bf16[1,1024,1,512]{3,2,0,1:T(2,128)(2,1)} reshape(bf16[2,1,512,1,4,128]{5,4,2,0,3,1:T(4,128)(2,1)} %get-tuple-element.66) | data formatting | bytes 2097152 | tf_op jit(solution)/shard_map/reshape;vmap()/reshape;vmap()/transpose | solution.py:132
  173.6 9.0 %reduce.8 = bf16[1024,512]{1,0:T(8,128)(2,1)} reduce(bf16[1024,1,1,512]{3,2,1,0:T(2,128)(2,1)} %bitcast.265, bf16[]{:T(256)} %broadcast.143), dimensions={1,2}, to_apply=%bitcast.178.reduce_sub_computation | reduce | bytes 2097154
  182.6 2.6 reshape.289
  186.2 1.1 copy.139
  187.4 4.8 all-to-all-start.5
  192.3 1.9 reshape.292
  194.1 1.1 copy.138
  198.9 1.6 convolution_multiply_fusion.3
  200.5 1.5 convolution_multiply_fusion.4
  202.0 5.4 %all-to-all-done.5 = bf16[8,2,32768]{2,1,0:T(2,128)(2,1)} async-done(((bf16[8,2,32768]{2,1,0:T(2,128)(2,1)}), bf16[8,2,32768]{2,1,0:T(2,128)(2,1)}, u32[]{:S(2)}, u32[]{:S(2)}) %all-to-all-start.5) | async-done | bytes 1048608 | tf_op jit(solution)/shard_map/all_to_all | solution.py:131
  207.5 5.8 %reshape.290 = bf16[1024,1,1,512]{3,2,1,0:T(2,128)(2,1)} reshape(bf16[8,2,32768]{2,1,0:T(2,128)(2,1)} %all-to-all-done.5) | data formatting | bytes 2097152
  213.2 2.8 copy.137
  216.1 2.2 copy.116
  218.3 2.7 convolution_multiply_fusion.2
  221.0 1.7 convolution_convert_fusion
  222.7 5.2 %fusion.39 = f32[8192,192]{0,1:T(8,128)} fusion(bf16[1,128,8192]{2,1,0:T(8,128)(2,1)} %param.12, bf16[128,64]{0,1:T(8,128)(2,1)S(1)} %convolution_convert_fusion.1, bf16[128,64]{0,1:T(8,128)(2,1)S(1)} %convolution_convert_fusion.2, bf16[128,64]{0,1:T(8,128)(2,1)S(1)} %convolution_convert_fusion), kind=kOutput, calls=%fused_computation.45 | convolution fusion | flops 404373504 | bytes 8437760 | tf_op jit(solution)/shard_map/dot_general | solution.py:15
  229.5 2.3 copy.127
  231.7 273.1 %all-reduce.4.cloned.1.call-done = (f32[8192,192]{0,1:T(8,128)}, f32[64,4096]{1,0:T(8,128)}, f32[64,512]{1,0:T(8,128)}, f32[64,512]{1,0:T(8,128)}) async-done(((f32[8192,192]{0,1:T(8,128)}, f32[64,4096]{1,0:T(8,128)}, f32[64,512]{1,0:T(8,128)}, f32[64,512]{1,0:T(8,128)}), (f32[8192,192]{0,1:T(8,128)}, f32[64,4096]{1,0:T(8,128)}, f32[64,512]{1,0:T(8,128)}, f32[64,512]{1,0:T(8,128)})) %all-reduce.4.cloned.1.call-update) | async-done | bytes 7602192 | tf_op jit(solution)/shard_map/psum | solution.py:202
  506.5 2.3 copy.168
  508.8 1.6 copy.169
  510.3 1.6 copy.170
  (81 shorter events, 19.5 us)
Async XLA Ops:
  7.2 156.3 %copy-start = (bf16[8192,192]{0,1:T(8,128)(2,1)S(1)}, bf16[8192,192]{0,1:T(8,128)(2,1)}, u32[]{:S(2)}) copy-start(bf16[8192,192]{0,1:T(8,128)(2,1)} %param.18) | copy-start | bytes 9437188
  9.0 13.1 %all-to-all-start.1 = ((bf16[1,128,8,128]{3,1,0,2:T(8,128)(2,1)}), bf16[1,128,8,128]{3,1,0,2:T(8,128)(2,1)S(1)}, u32[]{:S(2)}, u32[]{:S(2)}) async-start(bf16[1,128,8,128]{3,1,0,2:T(8,128)(2,1)} %bitcast.283), calls=%async_computation.1 | async-start | bytes 524288 | tf_op jit(solution)/shard_map/all_to_all | solution.py:114
  15.6 52.1 %copy-start.9 = (bf16[1,128,512]{2,1,0:T(8,128)(2,1)S(1)}, bf16[1,128,512]{2,1,0:T(8,128)(2,1)}, u32[]{:S(2)}) copy-start(bf16[1,128,512]{2,1,0:T(8,128)(2,1)} %param.15) | copy-start | bytes 393220
  22.1 20.4 %all-to-all-start = ((bf16[1,128,8,512]{1,3,0,2:T(8,128)(2,1)}), bf16[1,128,8,512]{1,3,0,2:T(8,128)(2,1)}, u32[]{:S(2)}, u32[]{:S(2)}) async-start(bf16[1,128,8,512]{1,3,0,2:T(8,128)(2,1)} %bitcast.268), calls=%async_computation | async-start | bytes 2097152 | tf_op jit(solution)/shard_map/all_to_all | solution.py:113
  42.5 20.2 %all-to-all-start.2 = ((bf16[1,128,8,512]{1,3,0,2:T(8,128)(2,1)}), bf16[1,128,8,512]{1,3,0,2:T(8,128)(2,1)}, u32[]{:S(2)}, u32[]{:S(2)}) async-start(bf16[1,128,8,512]{1,3,0,2:T(8,128)(2,1)} %bitcast.269), calls=%async_computation.2 | async-start | bytes 2097152 | tf_op jit(solution)/shard_map/all_to_all | solution.py:118
  62.7 20.2 %all-to-all-start.4 = ((bf16[1,128,8,512]{1,3,0,2:T(8,128)(2,1)}), bf16[1,128,8,512]{1,3,0,2:T(8,128)(2,1)}, u32[]{:S(2)}, u32[]{:S(2)}) async-start(bf16[1,128,8,512]{1,3,0,2:T(8,128)(2,1)} %bitcast.267), calls=%async_computation.4 | async-start | bytes 2097152 | tf_op jit(solution)/shard_map/all_to_all | solution.py:119
  83.7 13.6 %all-to-all-start.3 = ((bf16[1,128,8,128]{3,1,0,2:T(8,128)(2,1)}), bf16[1,128,8,128]{3,1,0,2:T(8,128)(2,1)}, u32[]{:S(2)}, u32[]{:S(2)}) async-start(bf16[1,128,8,128]{3,1,0,2:T(8,128)(2,1)} %bitcast.282), calls=%async_computation.3 | async-start | bytes 524288 | tf_op jit(solution)/shard_map/all_to_all | solution.py:115
  102.4 2.5 copy-start.6
  102.4 2.5 copy-start.7
  107.9 5.7 %copy-start.8 = (f32[1,1024,1,128]{1,3,2,0:T(8,128)}, f32[1,1024,1,128]{1,3,2,0:T(8,128)S(1)}, u32[]{:S(2)}) copy-start(f32[1,1024,1,128]{1,3,2,0:T(8,128)S(1)} %fusion.94) | copy-start | bytes 1572868 | tf_op jit(solution)/shard_map/vmap()/while
  108.0 5.7 %copy-start.1 = (bf16[1,1024,1,4,128]{1,4,3,2,0:T(8,128)(2,1)S(1)}, bf16[1,1024,1,4,128]{1,4,3,2,0:T(8,128)(2,1)}, u32[]{:S(2)}) copy-start(bf16[1,1024,1,4,128]{1,4,3,2,0:T(8,128)(2,1)} %get-tuple-element.355) | copy-start | bytes 3145732 | tf_op jit(solution)/shard_map/vmap()/while
  108.0 5.7 %copy-start.2 = (f32[1,1024,1,128]{1,3,2,0:T(8,128)S(1)}, f32[1,1024,1,128]{1,3,2,0:T(8,128)}, u32[]{:S(2)}) copy-start(f32[1,1024,1,128]{1,3,2,0:T(8,128)} %get-tuple-element.336) | copy-start | bytes 1572868 | tf_op jit(solution)/shard_map/vmap()/while
  113.7 2.2 copy-start.4
  114.6 1.7 copy-start.3
  116.4 1.0 copy-start.5
  122.5 2.5 copy-start.6
  122.5 2.5 copy-start.7
  128.0 5.7 %copy-start.8 = (f32[1,1024,1,128]{1,3,2,0:T(8,128)}, f32[1,1024,1,128]{1,3,2,0:T(8,128)S(1)}, u32[]{:S(2)}) copy-start(f32[1,1024,1,128]{1,3,2,0:T(8,128)S(1)} %fusion.94) | copy-start | bytes 1572868 | tf_op jit(solution)/shard_map/vmap()/while
  128.0 5.7 %copy-start.1 = (bf16[1,1024,1,4,128]{1,4,3,2,0:T(8,128)(2,1)S(1)}, bf16[1,1024,1,4,128]{1,4,3,2,0:T(8,128)(2,1)}, u32[]{:S(2)}) copy-start(bf16[1,1024,1,4,128]{1,4,3,2,0:T(8,128)(2,1)} %get-tuple-element.355) | copy-start | bytes 3145732 | tf_op jit(solution)/shard_map/vmap()/while
  128.0 5.7 %copy-start.2 = (f32[1,1024,1,128]{1,3,2,0:T(8,128)S(1)}, f32[1,1024,1,128]{1,3,2,0:T(8,128)}, u32[]{:S(2)}) copy-start(f32[1,1024,1,128]{1,3,2,0:T(8,128)} %get-tuple-element.336) | copy-start | bytes 1572868 | tf_op jit(solution)/shard_map/vmap()/while
  133.7 2.2 copy-start.4
  134.7 1.7 copy-start.3
  136.4 1.0 copy-start.5
  144.0 14.7 %all-to-all-start.7 = ((bf16[8,2,8192]{2,1,0:T(2,128)(2,1)}), bf16[8,2,8192]{2,1,0:T(2,128)(2,1)S(1)}, u32[]{:S(2)}, u32[]{:S(2)}) async-start(bf16[8,2,8192]{2,1,0:T(2,128)(2,1)} %reshape.293), calls=%async_computation.7 | async-start | bytes 524288 | tf_op jit(solution)/shard_map/all_to_all | solution.py:145
  158.7 28.8 %all-to-all-start.6 = ((bf16[8,2,8192]{2,1,0:T(2,128)(2,1)}), bf16[8,2,8192]{2,1,0:T(2,128)(2,1)}, u32[]{:S(2)}, u32[]{:S(2)}) async-start(bf16[8,2,8192]{2,1,0:T(2,128)(2,1)} %reshape.291), calls=%async_computation.6 | async-start | bytes 524288 | tf_op jit(solution)/shard_map/all_to_all | solution.py:138
  187.4 20.0 %all-to-all-start.5 = ((bf16[8,2,32768]{2,1,0:T(2,128)(2,1)}), bf16[8,2,32768]{2,1,0:T(2,128)(2,1)}, u32[]{:S(2)}, u32[]{:S(2)}) async-start(bf16[8,2,32768]{2,1,0:T(2,128)(2,1)} %reshape.289), calls=%async_computation.5 | async-start | bytes 2097152 | tf_op jit(solution)/shard_map/all_to_all | solution.py:131
  192.3 312.6 %all-reduce.4.cloned.1.call-start = ((), (), s32[]{:S(2)}) async-start(), calls=%async_computation.8 | async-start | bytes 15204352 | tf_op jit(solution)/shard_map/psum | solution.py:202
Sparse Core Ops, SparseCore 0:
  228.1 276.7 all-reduce.3
where the time goes:
time: 522 us; the launch traced here: 519 us
  waiting for transfers between devices  312 us (60%)
  local copies, waits for them, and re-layouts  75.7 us (15%)
  matrix products  46.3 us (9%)
  starting transfers between devices  40.9 us (8%)
  other arithmetic  28.1 us (5%)
  between operations  14.2 us (3%)
    psum x1, waiting for transfers between devices, body(): lax.psum((down_term, up_term_q, up_term_k, up_term_v), ('dp', 'seq'))  273 us
    unnamed x24, local copies, waits for them, and re-layouts  35.9 us
    unnamed x5, other arithmetic  16 us
    all_to_all x1, waiting for transfers between devices, body(): lax.all_to_all(to_heads(saved_queries), 'seq', split_axis=2, concat_axis=...  13 us
    all_to_all x1, waiting for transfers between devices, body(): lax.all_to_all(to_heads(output_gradient), 'seq', split_axis=2, concat_axi...  12.9 us
    dot_general x2, matrix products, one_block(): jnp.einsum('qkgd,skd->kgqs', grad_blk, values_dev, preferred_element_type...  11.4 us
    dot_general x4, matrix products, contract_rows(): lax.dot_general(left, right, (((0,), (0,)), ((), ())), preferred_element_...  11 us
  transfers between devices with their start and end apart: 9, of which 6 were waited for; matrix products, arithmetic and copies ran while one was open for 14% of the time, Pallas kernels for 0%

commit v1 on v0

v1 whole, which is shorter than its diff:
```python
import math

import jax
import jax.numpy as jnp
from jax import lax
from jax.experimental import pallas as pl
from jax.experimental.pallas import tpu as pltpu
from jax.sharding import PartitionSpec as P

BF = jnp.bfloat16
F32 = jnp.float32
HEAD = 128
SCALE = HEAD**-0.5
LOG2_SCALE = SCALE * math.log2(math.e)
FACTOR = 0.25 / math.sqrt(32768)
NX, NY, NZ = 4, 4, 8
PAIR = 512


def dot(left, right, left_axis, right_axis):
    return lax.dot_general(
        left, right, (((left_axis,), (right_axis,)), ((), ())), preferred_element_type=F32
    )


def kernel(
    x_in, q_in, k_in, v_in, o_in, g_in, wd_in, wq_in, wk_in, wv_in,
    dq_out, dk_out, dv_out, down_out, upq_out, upk_out, upv_out,
    xv, wd, wq, wk, wv, qb, gb, kb, vb, gown, oown, deltas, down_act,
    xcols, scores, row_max, dq_acc, dq_rows, grads_out, grads_in, own_grads,
    kv_rows, mid_part, mid_sib, mid_all, down_part, down_y, down_z, down_zin,
    up_part, up_x, up_xsum, up_z, up_piece, up_y, up_final, up_slab, up_all,
    loc, sib_s, sib_r, kv_s, kv_r, x_s, x_r, gr_s, gr_r, mid_s, mid_r,
    dy_s, dy_r, dz_s, dz_r, ux_s, ux_r, uz_s, uz_r, uy_s, uy_r, az_s, az_r, ax_s, ax_r,
):
    dp = lax.axis_index("dp")
    seq = lax.axis_index("seq")
    x, z = dp // NZ, dp % NZ
    y, c = seq // 2, seq % 2
    oc = 1 - c

    def at(xx, yy, zz, cc):
        return {"dp": xx * NZ + zz, "seq": yy * 2 + cc}

    sibling = at(x, y, z, oc)

    def remote(src, dst, ssem, rsem, device):
        return pltpu.make_async_remote_copy(
            src_ref=src, dst_ref=dst, send_sem=ssem, recv_sem=rsem,
            device_id=device, device_id_type=pl.DeviceIdType.MESH,
        )

    def arrived(dst, rsem, ssem):
        remote(dst, dst, ssem, rsem, sibling).wait_recv()

    def part(start, size, unit):
        return pl.ds(pl.multiple_of(start * unit, unit), size)

    locals_ = []

    def local(src, dst, index):
        copy = pltpu.make_async_copy(src, dst, loc.at[index])
        copy.start()
        locals_.append(copy)
        return copy

    my_rows = part(c, 128, 128)
    c_gown = local(g_in.at[0], gown, 0)
    c_oown = local(o_in.at[0], oown, 1)
    c_q = local(q_in.at[0, :, part(c, 2048, 2048)], qb.at[my_rows], 2)
    c_g = local(g_in.at[0, :, part(c, 2048, 2048)], gb.at[my_rows], 3)
    chip_rows = part(seq, 128, 128)
    c_kv = []
    for g in range(2):
        head = part(2 * c + g, 128, 128)
        c_kv.append((
            local(k_in.at[0, :, head], kb.at[g, chip_rows], 4 + 2 * g),
            local(v_in.at[0, :, head], vb.at[g, chip_rows], 5 + 2 * g),
        ))
    c_x = local(x_in.at[0], xv, 8)
    c_wd = local(wd_in, wd, 9)
    c_xc = local(
        x_in.at[0, :, part(x * 2 + c, 1024, 1024)], xcols.at[part(x * 2 + c, 128, 128)], 10
    )
    c_wq = local(wq_in.at[:, part(c, 2048, 2048)], wq, 11)
    c_wk = local(wk_in.at[:, part(c, 256, 256)], wk, 12)
    c_wv = local(wv_in.at[:, part(c, 256, 256)], wv, 13)

    barrier = pltpu.get_barrier_semaphore()
    peers = [sibling]
    for cc in range(2):
        peers += [at(x, (y + d) % NY, z, cc) for d in range(1, NY)]
        peers += [at((x + d) % NX, y, z, cc) for d in range(1, NX)]
        peers += [at(x, y, (z + d) % NZ, cc) for d in range(1, NZ)]
    for peer in peers:
        pl.semaphore_signal(
            barrier, inc=1, device_id=peer, device_id_type=pl.DeviceIdType.MESH
        )
    pl.semaphore_wait(barrier, len(peers))

    started = []

    def send(src, dst, ssem, rsem, device):
        copy = remote(src, dst, ssem, rsem, device)
        copy.start()
        started.append(copy)

    def kv_copy(g, which, yy, cc):
        source, target = ((k_in, kb), (v_in, vb))[which]
        return remote(
            source.at[0, :, part(2 * cc + g, 128, 128)],
            target.at[g, chip_rows],
            kv_s.at[g, which, yy * 2 + cc],
            kv_r.at[g, which, seq],
            at(x, yy, z, cc),
        )

    def each_later(body):
        for d in range(1, NY):
            @pl.when(y + d < NY)
            def _():
                body(y + d)

    for g in range(2):
        send(q_in.at[0, :, part(oc * 2 + g, 1024, 1024)],
             qb.at[my_rows, g * 1024:(g + 1) * 1024], sib_s.at[g], sib_r.at[g], sibling)
        send(g_in.at[0, :, part(oc * 2 + g, 1024, 1024)],
             gb.at[my_rows, g * 1024:(g + 1) * 1024], sib_s.at[2 + g], sib_r.at[2 + g], sibling)
        for which in range(2):
            copy = kv_copy(g, which, y, oc)
            copy.start()
            started.append(copy)

            def go(yy, g=g, which=which):
                for cc in range(2):
                    kv_copy(g, which, yy, cc).start()

            each_later(go)
        if g == 0:
            for d in range(NX):
                for cc in ([oc] if d == 0 else [0, 1]):
                    xx = (x + d) % NX
                    send(x_in.at[0, :, part(xx * 2 + cc, 1024, 1024)],
                         xcols.at[part(x * 2 + c, 128, 128)],
                         x_s.at[xx * 2 + cc], x_r.at[x * 2 + c], at(xx, y, z, cc))

    c_gown.wait()
    c_oown.wait()
    pick = (
        lax.broadcasted_iota(jnp.int32, (8, 1024), 1) // 128
        == lax.broadcasted_iota(jnp.int32, (8, 1024), 0)
    ).astype(BF)
    for chunk in range(4):
        cols = slice(chunk * 1024, (chunk + 1) * 1024)
        product = gown[:, cols].astype(F32) * oown[:, cols].astype(F32)
        high = product.astype(BF)
        low = (product - high.astype(F32)).astype(BF)
        deltas[chunk] = dot(pick, high, 1, 1) + dot(pick, low, 1, 1)
    for g in range(2):
        send(deltas.at[oc * 2 + g], deltas.at[4 + 2 * c + g], sib_s.at[4 + g], sib_r.at[4 + g], sibling)

    c_x.wait()
    c_wd.wait()
    total = jnp.zeros((128, 192), F32)
    for chunk in range(4):
        cols = slice(chunk * 2048, (chunk + 1) * 2048)
        total += dot(xv[:, cols], wd[cols, :], 1, 0)
    down_act[my_rows, :] = total.astype(BF)
    send(down_act.at[my_rows], down_act.at[my_rows], sib_s.at[6], sib_r.at[6], sibling)

    c_q.wait()
    c_g.wait()
    other_rows = part(oc, 128, 128)
    chip = part(y, 256, 256)

    def pair_of(ref, g, h):
        first = (g * 8 + h) * 128
        return jnp.concatenate(
            [ref[:, first:first + 128], ref[:, first + 128:first + 256]], axis=0
        )

    for g in range(2):
        arrived(qb.at[other_rows, g * 1024:(g + 1) * 1024], sib_r.at[g], sib_s.at[g])
        sib_rows = part(y * 2 + oc, 128, 128)
        c_kv[g][0].wait()
        arrived(kb.at[g, sib_rows], kv_r.at[g, 0, y * 2 + oc], kv_s.at[g, 0, 0])

        def scores_of(j, first, g=g):
            rows = part(j, 256, 256)
            keys = kb[g, rows, :]
            for h in range(0, 8, 2):
                qs = slice(h * 256, h * 256 + PAIR)
                s = dot(keys, pair_of(qb, g, h), 1, 1)
                if first:
                    key_at = lax.broadcasted_iota(jnp.int32, (256, PAIR), 0)
                    query_at = lax.broadcasted_iota(jnp.int32, (256, PAIR), 1) % 256
                    s = jnp.where(key_at <= query_at, s, -jnp.inf)
                scores[rows, qs] = s
                top = jnp.max(s, axis=0, keepdims=True)
                row_max[:, qs] = top if first else jnp.maximum(row_max[:, qs], top)

        scores_of(y, True)

        def more_scores(t, carry, g=g):
            j = y - 1 - t
            for cc in range(2):
                arrived(kb.at[g, part(j * 2 + cc, 128, 128)], kv_r.at[g, 0, j * 2 + cc], kv_s.at[g, 0, 0])
            scores_of(j, False)
            return carry

        lax.fori_loop(0, y, more_scores, 0)
        row_max[...] = row_max[...] * LOG2_SCALE

        def weights_of(j, sums):
            rows = part(j, 256, 256)
            found = []
            for h in range(0, 8, 2):
                qs = slice(h * 256, h * 256 + PAIR)
                w = jnp.exp2(scores[rows, qs] * LOG2_SCALE - row_max[:, qs])
                scores[rows, qs] = w
                found.append(jnp.sum(w, axis=0, keepdims=True))
            return sums + jnp.concatenate(found, axis=1)

        sums = lax.fori_loop(0, y + 1, weights_of, jnp.zeros((1, 2048), F32))
        row_max[...] = 1.0 / sums
        dq_acc[...] = jnp.zeros_like(dq_acc)

        arrived(gb.at[other_rows, g * 1024:(g + 1) * 1024], sib_r.at[2 + g], sib_s.at[2 + g])
        arrived(deltas.at[4 + 2 * oc + g], sib_r.at[4 + g], sib_s.at[4 + g])
        c_kv[g][1].wait()
        arrived(vb.at[g, sib_rows], kv_r.at[g, 1, y * 2 + oc], kv_s.at[g, 1, 0])
        mine = deltas[2 * c + g]
        theirs = deltas[4 + 2 * oc + g]
        low_half = jnp.where(c == 0, mine, theirs)
        high_half = jnp.where(c == 0, theirs, mine)
        delta_rows = [
            jnp.concatenate([low_half[h:h + 1], high_half[h:h + 1]], axis=1) for h in range(8)
        ]

        def grads_of(j, g=g, delta_rows=delta_rows):
            rows = part(j, 256, 256)
            keys, values = kb[g, rows, :], vb[g, rows, :]
            keys_t = keys.T
            value_sum = jnp.zeros((256, 128), F32)
            key_sum = jnp.zeros((256, 128), F32)
            for h in range(0, 8, 2):
                qs = slice(h * 256, h * 256 + PAIR)
                grad, query = pair_of(gb, g, h), pair_of(qb, g, h)
                prob_grad = dot(values, grad, 1, 1)
                prob = scores[rows, qs] * row_max[:, qs]
                delta = jnp.concatenate([delta_rows[h], delta_rows[h + 1]], axis=1)
                score_grad = (prob * (prob_grad - delta)).astype(BF)
                value_sum = value_sum + dot(prob.astype(BF), grad, 1, 0)
                key_sum = key_sum + dot(score_grad, query, 1, 0)
                dq_acc[:, qs] += dot(keys_t, score_grad, 1, 0)
            return key_sum * SCALE, value_sum

        def far_grads(j, carry, g=g):
            for cc in range(2):
                arrived(vb.at[g, part(j * 2 + cc, 128, 128)], kv_r.at[g, 1, j * 2 + cc], kv_s.at[g, 1, 0])
            key_sum, value_sum = grads_of(j)
            grads_out[g, j, 0] = key_sum.astype(BF)
            grads_out[g, j, 1] = value_sum.astype(BF)
            remote(grads_out.at[g, j], grads_in.at[g, y], gr_s.at[g, j], gr_r.at[g, y], at(x, j, z, c)).start()
            return carry

        lax.fori_loop(0, y, far_grads, 0)
        key_sum, value_sum = grads_of(y)
        own_grads[g, 0] = key_sum
        own_grads[g, 1] = value_sum
        for h in range(8):
            first = (g * 8 + h) * 128
            dq_rows[:, first:first + 128] = (
                dq_acc[:, h * 256:(h + 1) * 256].T * SCALE
            ).astype(BF)
        span = slice(g * 1024, (g + 1) * 1024)
        there = part(c * 2 + g, 1024, 1024)
        local(dq_rows.at[my_rows, span], dq_out.at[0, :, there], 14 + g)
        send(dq_rows.at[other_rows, span], dq_out.at[0, :, there], sib_s.at[7 + g], sib_r.at[7 + g], sibling)

    c_wq.wait()
    mid_part[:, 0:64] = dot(dq_rows[...], wq[...], 1, 1)
    arrived(down_act.at[other_rows], sib_r.at[6], sib_s.at[6])
    up_q = dot(down_act[:, 0:64], dq_rows[...], 0, 0).astype(BF)
    for k in range(NX):
        up_part[k, :, 0:2048] = up_q[k * 16:(k + 1) * 16, :]
        up_part[k, :, 2560:3072] = jnp.zeros((16, 512), BF)

    c_wk.wait()
    c_wv.wait()
    for g in range(2):
        def add_later(yy, g=g):
            arrived(grads_in.at[g, yy], gr_r.at[g, yy], gr_s.at[g, 0])
            for which in range(2):
                own_grads[g, which] = own_grads[g, which] + grads_in[g, yy, which].astype(F32)

        each_later(add_later)
        for which in range(2):
            kv_rows[which, :, g * 128:(g + 1) * 128] = own_grads[g, which].astype(BF)
    there = part(c, 256, 256)
    for which, out in ((0, dk_out), (1, dv_out)):
        local(kv_rows.at[which, my_rows], out.at[0, :, there], 16 + which)
        send(kv_rows.at[which, other_rows], out.at[0, :, there],
             sib_s.at[9 + which], sib_r.at[9 + which], sibling)
        weight = (wk, wv)[which]
        mid_part[:, 64 + 64 * which:128 + 64 * which] = dot(kv_rows[which], weight[...], 1, 1)
    send(mid_part, mid_sib, sib_s.at[11], sib_r.at[11], sibling)
    for which in range(2):
        up = dot(down_act[:, 64 + 64 * which:128 + 64 * which], kv_rows[which], 0, 0).astype(BF)
        for k in range(NX):
            up_part[k, :, 2048 + 256 * which:2304 + 256 * which] = up[k * 16:(k + 1) * 16, :]
    for d in range(1, NX):
        xx = (x + d) % NX
        send(up_part.at[xx], up_x.at[x], ux_s.at[xx], ux_r.at[x], at(xx, y, z, c))

    arrived(mid_sib, sib_r.at[11], sib_s.at[11])
    chip_tokens = part(x, 256, 256)
    mid_all[chip_tokens, :] = (mid_part[...] + mid_sib[...]).astype(BF)
    for d in range(1, NX):
        xx = (x + d) % NX
        send(mid_all.at[chip_tokens], mid_all.at[chip_tokens], mid_s.at[xx], mid_r.at[x], at(xx, y, z, c))

    up_x[x] = up_part[x]
    for d in range(1, NX):
        xx = (x + d) % NX
        arrived(up_x.at[xx], ux_r.at[xx], ux_s.at[0])
    summed = jnp.zeros((16, 3072), F32)
    for k in range(NX):
        summed = summed + up_x[k].astype(F32)
    summed = summed.astype(BF)
    for k in range(NZ):
        up_xsum[k] = summed[:, k * 384:(k + 1) * 384]
    for d in range(1, NZ):
        zz = (z + d) % NZ
        send(up_xsum.at[zz], up_z.at[z], uz_s.at[zz], uz_r.at[z], at(x, y, zz, c))

    c_xc.wait()
    for d in range(NX):
        xx = (x + d) % NX
        if d:
            arrived(mid_all.at[part(xx, 256, 256)], mid_r.at[xx], mid_s.at[0])
        for cc in ([oc] if d == 0 else [0, 1]):
            arrived(xcols.at[part(xx * 2 + cc, 128, 128)], x_r.at[xx * 2 + cc], x_s.at[0])
    mids = mid_all[...]
    for zz in range(4):
        found = dot(mids, xcols[:, zz * 256:(zz + 1) * 256], 0, 0).T
        for yy in range(NY):
            down_part[yy, zz] = found[yy * 64:(yy + 1) * 64, :].astype(BF)
    for d in range(1, NY):
        yy = (y + d) % NY
        send(down_part.at[yy], down_y.at[y], dy_s.at[yy], dy_r.at[y], at(x, yy, z, c))

    up_z[z] = up_xsum[z]
    for d in range(1, NZ):
        zz = (z + d) % NZ
        arrived(up_z.at[zz], uz_r.at[zz], uz_s.at[0])
    piece = jnp.zeros((16, 384), F32)
    for k in range(NZ):
        piece = piece + up_z[k].astype(F32)
    up_piece[...] = piece.astype(BF)
    up_y[y] = up_piece[...]
    for d in range(1, NY):
        yy = (y + d) % NY
        send(up_piece, up_y.at[y], uy_s.at[yy], uy_r.at[y], at(x, yy, z, c))

    down_y[y] = down_part[y]
    for d in range(1, NY):
        yy = (y + d) % NY
        arrived(down_y.at[yy], dy_r.at[yy], dy_s.at[0])
    part_sum = jnp.zeros((4, 64, 192), F32)
    for k in range(NY):
        part_sum = part_sum + down_y[k].astype(F32)
    down_z[...] = part_sum.astype(BF)
    for k in range(4):
        for cc in range(2):
            zz = 4 * c + k
            src = down_z.at[k, cc * 32:(cc + 1) * 32]

            @pl.when(jnp.logical_or(zz != z, cc != c))
            def _():
                remote(src, down_zin.at[z], dz_s.at[k, cc], dz_r.at[z], at(x, y, zz, cc)).start()

    for d in range(1, NY):
        yy = (y + d) % NY
        arrived(up_y.at[yy], uy_r.at[yy], uy_s.at[0])
    final = jnp.zeros((16, 384), F32)
    for k in range(NY):
        final = final + up_y[k].astype(F32)
    up_final[z] = (final * FACTOR).astype(BF)
    for d in range(1, NZ):
        zz = (z + d) % NZ
        send(up_final.at[z], up_final.at[z], az_s.at[zz], az_r.at[z], at(x, y, zz, c))

    source_core = z // 4

    @pl.when(source_core == c)
    def _():
        down_zin[z] = down_z[z % 4, part(c, 32, 32), :]

    for d in range(NZ):
        zz = (z + d) % NZ
        if d == 0:
            @pl.when(source_core != c)
            def _():
                arrived(down_zin.at[zz], dz_r.at[zz], dz_s.at[0, 0])
        else:
            arrived(down_zin.at[zz], dz_r.at[zz], dz_s.at[0, 0])
    down = jnp.zeros((32, 192), F32)
    for k in range(NZ):
        down = down + down_zin[k].astype(F32)
    down_out[...] = down * FACTOR

    for d in range(1, NZ):
        zz = (z + d) % NZ
        arrived(up_final.at[zz], az_r.at[zz], az_s.at[0])
    for k in range(NZ):
        up_slab[:, k * 384:(k + 1) * 384] = up_final[k]
    up_all[c, x] = up_slab[...]
    for d in range(1, NX):
        xx = (x + d) % NX
        send(up_slab, up_all.at[c, x], ax_s.at[xx], ax_r.at[x], at(xx, y, z, c))
    for d in range(1, NX):
        xx = (x + d) % NX
        arrived(up_all.at[c, xx], ax_r.at[xx], ax_s.at[0])
    send(up_all.at[c], up_all.at[c], sib_s.at[12], sib_r.at[12], sibling)
    arrived(up_all.at[oc], sib_r.at[12], sib_s.at[12])
    for cc in range(2):
        for k in range(NX):
            rows = slice(k * 16, (k + 1) * 16)
            upq_out[rows, cc * 2048:(cc + 1) * 2048] = up_all[cc, k, :, 0:2048].astype(F32)
            upk_out[rows, cc * 256:(cc + 1) * 256] = up_all[cc, k, :, 2048:2304].astype(F32)
            upv_out[rows, cc * 256:(cc + 1) * 256] = up_all[cc, k, :, 2304:2560].astype(F32)

    for copy in locals_[14:]:
        copy.wait()
    for g in range(2):
        there = part(oc * 2 + g, 1024, 1024)
        arrived(dq_out.at[0, :, there], sib_r.at[7 + g], sib_s.at[7 + g])
    there = part(oc, 256, 256)
    arrived(dk_out.at[0, :, there], sib_r.at[9], sib_s.at[9])
    arrived(dv_out.at[0, :, there], sib_r.at[10], sib_s.at[10])
    for copy in started:
        copy.wait_send()
    for g in range(2):
        for which in range(2):
            def sent(yy, g=g, which=which):
                for cc in range(2):
                    kv_copy(g, which, yy, cc).wait_send()

            each_later(sent)

        def grads_sent(j, carry, g=g):
            remote(grads_out.at[g, j], grads_in.at[g, y], gr_s.at[g, j], gr_r.at[g, y], at(x, j, z, c)).wait_send()
            return carry

        lax.fori_loop(0, y, grads_sent, 0)
    for k in range(4):
        for cc in range(2):
            zz = 4 * c + k
            src = down_z.at[k, cc * 32:(cc + 1) * 32]

            @pl.when(jnp.logical_or(zz != z, cc != c))
            def _():
                remote(src, down_zin.at[z], dz_s.at[k, cc], dz_r.at[z], at(x, y, zz, cc)).wait_send()


def body(x_in, q_in, k_in, v_in, o_in, g_in, wd, wq, wk, wv):
    vm = pltpu.VMEM
    dma = pltpu.SemaphoreType.DMA
    any_ = pl.BlockSpec(memory_space=pl.ANY)
    vmem = pl.BlockSpec(memory_space=pltpu.VMEM)
    shape = jax.ShapeDtypeStruct
    scratch = [
        vm((128, 8192), BF), vm((8192, 192), BF), vm((64, 2048), BF), vm((64, 256), BF),
        vm((64, 256), BF), vm((256, 2048), BF), vm((256, 2048), BF), vm((2, 1024, 128), BF),
        vm((2, 1024, 128), BF), vm((128, 4096), BF), vm((128, 4096), BF), vm((8, 8, 128), F32),
        vm((256, 192), BF),
        vm((1024, 1024), BF), vm((1024, 2048), F32), vm((1, 2048), F32), vm((128, 2048), F32),
        vm((256, 2048), BF), vm((2, 4, 2, 256, 128), BF), vm((2, 4, 2, 256, 128), BF),
        vm((2, 2, 256, 128), F32),
        vm((2, 256, 256), BF), vm((256, 192), F32), vm((256, 192), F32), vm((1024, 192), BF),
        vm((4, 4, 64, 192), BF), vm((4, 4, 64, 192), BF), vm((4, 64, 192), BF), vm((8, 32, 192), BF),
        vm((4, 16, 3072), BF), vm((4, 16, 3072), BF), vm((8, 16, 384), BF), vm((8, 16, 384), BF),
        vm((16, 384), BF), vm((4, 16, 384), BF), vm((8, 16, 384), BF), vm((16, 3072), BF),
        vm((2, 4, 16, 3072), BF),
        dma((18,)), dma((13,)), dma((13,)), dma((2, 2, 8)), dma((2, 2, 8)), dma((8,)), dma((8,)),
        dma((2, 4)), dma((2, 4)), dma((4,)), dma((4,)),
        dma((4,)), dma((4,)), dma((4, 2)), dma((8,)), dma((4,)), dma((4,)), dma((8,)), dma((8,)),
        dma((4,)), dma((4,)), dma((8,)), dma((8,)), dma((4,)), dma((4,)),
    ]
    return pl.pallas_call(
        kernel,
        out_shape=[
            shape((1, 128, 4096), BF), shape((1, 128, 512), BF), shape((1, 128, 512), BF),
            shape((32, 192), F32), shape((64, 4096), F32), shape((64, 512), F32),
            shape((64, 512), F32),
        ],
        in_specs=[any_] * 10,
        out_specs=[any_] * 3 + [vmem] * 4,
        scratch_shapes=scratch,
        compiler_params=pltpu.CompilerParams(
            vmem_limit_bytes=52 * 2**20, collective_id=0, has_side_effects=True
        ),
        cost_estimate=pl.CostEstimate(
            flops=8 * 10**9, bytes_accessed=12 * 2**20, transcendentals=4 * 2**20
        ),
    )(x_in, q_in, k_in, v_in, o_in, g_in, wd, wq, wk, wv)


def solution(mesh):
    token = P("dp", "seq", None)
    return jax.shard_map(
        body,
        mesh=mesh,
        in_specs=(token,) * 6 + (P(),) * 4,
        out_specs=(token,) * 3 + (P(("dp", "seq"), None), P(), P(), P()),
        check_vma=False,
    )
```

time: 522 us -> 93 us (0.18)
  waiting for transfers between devices: 312 us -> 0 us
  Pallas kernels: 0 us -> 79.5 us
  local copies, waits for them, and re-layouts: 75.7 us -> 12.6 us
  matrix products: 46.3 us -> 0 us
  starting transfers between devices: 40.9 us -> 0 us
  other arithmetic: 28.1 us -> 0 us
  between operations: 14.2 us -> 0.71 us
    psum x1 -> x0, waiting for transfers between devices: 273 us -> none  [body(): lax.psum((down_term, up_term_q, up_term_k, up_term_v), ('dp', 'seq'))]
    pallas_call x0 -> x1, Pallas kernels: none -> 79.5 us  [body(): pl.pallas_call(kernel, out_shape=[shape((1, 128, 4096), BF), shape((1, 12...]
    dot_general x18 -> x0, matrix products: 46.3 us -> none  [the longest x2 11.4 us: one_block(): jnp.einsum('qkgd,skd->kgqs', grad_blk, values_dev, preferred_element_type...]
    all_to_all x8 -> x0, starting transfers between devices: 40.9 us -> none  [the longest x1 6.55 us: body(): lax.all_to_all(to_heads(widen(saved_keys)), 'seq', split_axis=2, concat_a...]
    all_to_all x8 -> x0, waiting for transfers between devices: 38.8 us -> none  [the longest x1 13 us: body(): lax.all_to_all(to_heads(saved_queries), 'seq', split_axis=2, concat_axis=...]
    unnamed x24 -> x20, local copies, waits for them, and re-layouts: 35.9 us -> 12.6 us
    unnamed x5 -> x0, other arithmetic: 16 us -> none
    all_to_all x3 -> x0, local copies, waits for them, and re-layouts: 7.99 us -> none  [the longest x1 2.87 us: body(): lax.all_to_all(to_heads(saved_queries), 'seq', split_axis=2, concat_axis=...]
  transfers between devices with their start and end apart: 9 -> 0, of which waited for: 6 -> 0; matrix products, arithmetic and copies ran while one was open for 14% -> 0% of each run, Pallas kernels for 0% -> 0%
where the time goes in v1:
time: 93 us; the launch traced here: 92.8 us
  Pallas kernels  79.5 us (85%)
  local copies, waits for them, and re-layouts  12.6 us (14%)
    pallas_call x1, Pallas kernels, body(): pl.pallas_call(kernel, out_shape=[shape((1, 128, 4096), BF), shape((1, 12...  79.5 us
    unnamed x20, local copies, waits for them, and re-layouts  12.6 us

profile of v1, /device:TPU:1, one launch (start us, length us, event | category | flops | bytes accessed | tf_op | source)
XLA Modules:
  0.0 92.8 jit_solution(12380326334836866755)
XLA Ops:
  0.6 0.0 copy-start.4
  0.6 0.0 copy-start.3
  0.7 0.0 copy-start
  0.7 0.0 copy-start.2
  0.7 0.0 copy-start.1
  0.7 6.0 %copy.17.wd_in = bf16[8192,192]{1,0:T(8,128)(2,1)} copy(bf16[8192,192]{0,1:T(8,128)(2,1)} %param.16) | data formatting | bytes 6291456 | tf_op args[6]
  6.7 0.0 copy-done.4
  6.7 0.0 copy-done.3
  6.7 0.0 copy-done
  6.7 0.0 copy-done.2
  6.7 0.0 copy-done.1
  6.7 79.5 %shard_map.153 = (bf16[1,128,4096]{2,1,0:T(8,128)(2,1)}, bf16[1,128,512]{2,1,0:T(8,128)(2,1)S(1)}, bf16[1,128,512]{2,1,0:T(8,128)(2,1)S(1)}, f32[32,192]{1,0:T(8...) custom-call(bf16[1,128,8192]{2,1,0:T(8,128)(2,1)} %x_in.1, ...), custom_call_target="tpu_custom_call" | custom-call | flops 8000000000 | bytes 12582912 | tf_op jit(solution)/shard_map/pallas_call | solution.py:491
  86.2 0.0 copy-start.5
  86.2 2.4 %copy.25 = bf16[1,128,4096]{2,1,0:T(8,128)(2,1)} copy(bf16[1,128,4096]{2,1,0:T(8,128)(2,1)} %get-tuple-element.14) | data formatting | bytes 2097152
  88.6 0.7 copy.26
  89.2 0.7 copy.27
  89.9 0.6 copy.28
  90.5 0.0 copy-done.5
  90.5 1.0 %copy.29 = f32[64,4096]{1,0:T(8,128)} copy(f32[64,4096]{1,0:T(8,128)S(1)} %copy-done.5) | data formatting | bytes 2097152
  91.5 0.7 copy.30
  92.1 0.7 copy.31
Async XLA Ops:
  0.6 6.1 %copy-start.4 = (bf16[64,512]{1,0:T(8,128)(2,1)S(1)}, bf16[64,512]{1,0:T(8,128)(2,1)}, u32[]{:S(2)}) copy-start(bf16[64,512]{1,0:T(8,128)(2,1)} %wv_in.1) | copy-start | bytes 196612
  0.6 6.1 %copy-start.3 = (bf16[64,512]{1,0:T(8,128)(2,1)S(1)}, bf16[64,512]{1,0:T(8,128)(2,1)}, u32[]{:S(2)}) copy-start(bf16[64,512]{1,0:T(8,128)(2,1)} %wk_in.1) | copy-start | bytes 196612
  0.7 6.1 %copy-start = (bf16[64,4096]{1,0:T(8,128)(2,1)S(1)}, bf16[64,4096]{1,0:T(8,128)(2,1)}, u32[]{:S(2)}) copy-start(bf16[64,4096]{1,0:T(8,128)(2,1)} %wq_in.1) | copy-start | bytes 1572868
  0.7 6.1 %copy-start.2 = (bf16[1,128,512]{2,1,0:T(8,128)(2,1)S(1)}, bf16[1,128,512]{2,1,0:T(8,128)(2,1)}, u32[]{:S(2)}) copy-start(bf16[1,128,512]{2,1,0:T(8,128)(2,1)} %v_in.1) | copy-start | bytes 393220
  0.7 6.1 %copy-start.1 = (bf16[1,128,512]{2,1,0:T(8,128)(2,1)S(1)}, bf16[1,128,512]{2,1,0:T(8,128)(2,1)}, u32[]{:S(2)}) copy-start(bf16[1,128,512]{2,1,0:T(8,128)(2,1)} %k_in.1) | copy-start | bytes 393220
  86.2 4.3 %copy-start.5 = (f32[64,4096]{1,0:T(8,128)S(1)}, f32[64,4096]{1,0:T(8,128)}, u32[]{:S(2)}) copy-start(f32[64,4096]{1,0:T(8,128)} %get-tuple-element.18) | copy-start | bytes 3145732

commit v2 on v1

v2 whole, which is shorter than its diff:
```python
import math

import jax
import jax.numpy as jnp
from jax import lax
from jax.experimental import pallas as pl
from jax.experimental.pallas import tpu as pltpu
from jax.sharding import PartitionSpec as P

BF = jnp.bfloat16
F32 = jnp.float32
HEAD = 128
SCALE = HEAD**-0.5
LOG2_SCALE = SCALE * math.log2(math.e)
FACTOR = 0.25 / math.sqrt(32768)
NX, NY, NZ = 4, 4, 8
ROWS = 2048


def dot(left, right, left_axis, right_axis):
    return lax.dot_general(
        left, right, (((left_axis,), (right_axis,)), ((), ())), preferred_element_type=F32
    )


def kernel(
    x_in, q_in, k_in, v_in, o_in, g_in, wd_in, wq_in, wk_in, wv_in,
    dq_out, dk_out, dv_out, down_out, up_out,
    xv, wd, wq, wk, wv, qb, gb, kb, vb, gown, oown, deltas, down_act,
    xcols, scores, row_max, delta_rows, dq_acc, dq_rows, grads_out, grads_in, own_grads,
    kv_rows, mid_part, mid_sib, mid_all, down_part, down_y, down_z, down_zin,
    up_part, up_y, up_sum, up_rs, up_fin,
    loc, sib_s, sib_r, kv_s, kv_r, x_s, x_r, gr_s, gr_r, mid_s, mid_r, fwd_s, fwd_r,
    dy_s, dy_r, dz_s, dz_r, uy_s, uy_r, us_s, us_r, ag_s, ag_r, ay_s, ay_r, sh_s, sh_r,
):
    dp = lax.axis_index("dp")
    seq = lax.axis_index("seq")
    x, z = dp // NZ, dp % NZ
    y, c = seq // 2, seq % 2
    oc = 1 - c

    def at(xx, yy, zz, cc):
        return {"dp": xx * NZ + zz, "seq": yy * 2 + cc}

    sibling = at(x, y, z, oc)

    def remote(src, dst, ssem, rsem, device):
        return pltpu.make_async_remote_copy(
            src_ref=src, dst_ref=dst, send_sem=ssem, recv_sem=rsem,
            device_id=device, device_id_type=pl.DeviceIdType.MESH,
        )

    def arrived(dst, rsem, ssem):
        remote(dst, dst, ssem, rsem, sibling).wait_recv()

    def part(start, size, unit):
        return pl.ds(pl.multiple_of(start * unit, unit), size)

    locals_ = []

    def local(src, dst, index):
        copy = pltpu.make_async_copy(src, dst, loc.at[index])
        copy.start()
        locals_.append(copy)
        return copy

    my_rows = part(c, 128, 128)
    c_gown = local(g_in.at[0], gown, 0)
    c_oown = local(o_in.at[0], oown, 1)
    c_q = local(q_in.at[0, :, part(c, 2048, 2048)], qb.at[my_rows], 2)
    c_g = local(g_in.at[0, :, part(c, 2048, 2048)], gb.at[my_rows], 3)
    chip_rows = part(seq, 128, 128)
    c_kv = []
    for g in range(2):
        head = part(2 * c + g, 128, 128)
        c_kv.append((
            local(k_in.at[0, :, head], kb.at[g, chip_rows], 4 + 2 * g),
            local(v_in.at[0, :, head], vb.at[g, chip_rows], 5 + 2 * g),
        ))
    c_x = local(x_in.at[0], xv, 8)
    c_wd = local(wd_in, wd, 9)
    c_xc = local(
        x_in.at[0, :, part(x * 2 + c, 1024, 1024)], xcols.at[part(x * 2 + c, 128, 128)], 10
    )
    c_wq = local(wq_in.at[:, part(c, 2048, 2048)], wq, 11)
    c_wk = local(wk_in.at[:, part(c, 256, 256)], wk, 12)
    c_wv = local(wv_in.at[:, part(c, 256, 256)], wv, 13)

    barrier = pltpu.get_barrier_semaphore()

    def greet(device):
        pl.semaphore_signal(
            barrier, inc=1, device_id=device, device_id_type=pl.DeviceIdType.MESH
        )

    greet(sibling)
    for d in range(1, NY):
        for cc in range(2):
            greet(at(x, (y + d) % NY, z, cc))
    for d in range(1, NX):
        greet(at((x + d) % NX, y, z, oc))
    for d in range(1, NZ):
        greet(at(x, y, (z + d) % NZ, oc))
    for d in range(1, NX * NZ):
        greet({"dp": (dp + d) % (NX * NZ), "seq": seq})
    pl.semaphore_wait(barrier, 1 + 2 * (NY - 1) + NX - 1 + NZ - 1 + NX * NZ - 1)

    started = []

    def send(src, dst, ssem, rsem, device):
        copy = remote(src, dst, ssem, rsem, device)
        copy.start()
        started.append(copy)

    def kv_copy(g, which, yy, cc):
        source, target = ((k_in, kb), (v_in, vb))[which]
        return remote(
            source.at[0, :, part(2 * cc + g, 128, 128)],
            target.at[g, chip_rows],
            kv_s.at[g, which, yy * 2 + cc],
            kv_r.at[g, which, seq],
            at(x, yy, z, cc),
        )

    def each_later(body):
        for d in range(1, NY):
            @pl.when(y + d < NY)
            def _():
                body(y + d)

    def send_kv(g, which):
        copy = kv_copy(g, which, y, oc)
        copy.start()
        started.append(copy)

        def go(yy):
            for cc in range(2):
                kv_copy(g, which, yy, cc).start()

        each_later(go)

    def span_of(g):
        return part(g, 1024, 1024)

    send_kv(0, 0)
    for g in range(2):
        send(q_in.at[0, :, span_of(oc * 2 + g)], qb.at[my_rows, span_of(g)],
             sib_s.at[g], sib_r.at[g], sibling)

    c_gown.wait()
    c_oown.wait()
    pick = (
        lax.broadcasted_iota(jnp.int32, (8, 1024), 1) // 128
        == lax.broadcasted_iota(jnp.int32, (8, 1024), 0)
    ).astype(BF)
    for chunk in range(4):
        if chunk == 2:
            send_kv(1, 0)
        cols = slice(chunk * 1024, (chunk + 1) * 1024)
        product = gown[:, cols].astype(F32) * oown[:, cols].astype(F32)
        high = product.astype(BF)
        low = (product - high.astype(F32)).astype(BF)
        deltas[chunk] = dot(pick, high, 1, 1) + dot(pick, low, 1, 1)
    for g in range(2):
        send(deltas.at[oc * 2 + g], deltas.at[4 + 2 * c + g], sib_s.at[4 + g], sib_r.at[4 + g], sibling)

    send_kv(0, 1)
    for g in range(2):
        send(g_in.at[0, :, span_of(oc * 2 + g)], gb.at[my_rows, span_of(g)],
             sib_s.at[2 + g], sib_r.at[2 + g], sibling)
    c_x.wait()
    c_wd.wait()
    total = jnp.zeros((128, 192), F32)
    for chunk in range(4):
        cols = slice(chunk * 2048, (chunk + 1) * 2048)
        total += dot(xv[:, cols], wd[:, cols], 1, 1)
    down_act[my_rows, :] = total.astype(BF)
    send(down_act.at[my_rows], down_act.at[my_rows], sib_s.at[6], sib_r.at[6], sibling)
    send_kv(1, 1)
    for d in range(NX):
        for cc in ([oc] if d == 0 else [0, 1]):
            xx = (x + d) % NX
            send(x_in.at[0, :, part(xx * 2 + cc, 1024, 1024)],
                 xcols.at[part(x * 2 + c, 128, 128)],
                 x_s.at[xx * 2 + cc], x_r.at[x * 2 + c], at(xx, y, z, cc))

    c_q.wait()
    c_g.wait()
    other_rows = part(oc, 128, 128)

    def heads_of(ref, g):
        return jnp.concatenate(
            [ref[:, part(g * 8 + h, 128, 128)] for h in range(8)], axis=0
        )

    sib_rows = part(y * 2 + oc, 128, 128)
    for g in range(2):
        c_kv[g][0].wait()
        c_kv[g][1].wait()

    def scores_of(g, j, first):
        rows = part(j, 256, 256)
        s = dot(kb[g, rows, :], heads_of(qb, g), 1, 1)
        if first:
            key_at = lax.broadcasted_iota(jnp.int32, (256, ROWS), 0)
            query_at = lax.broadcasted_iota(jnp.int32, (256, ROWS), 1) % 256
            s = jnp.where(key_at <= query_at, s, -jnp.inf)
        scores[g, rows, :] = s
        top = jnp.max(s, axis=0, keepdims=True)
        row_max[g] = top if first else jnp.maximum(row_max[g], top)

    def own_scores(g, carry):
        arrived(qb.at[other_rows, span_of(g)], sib_r.at[g], sib_s.at[g])
        arrived(kb.at[g, sib_rows], kv_r.at[g, 0, y * 2 + oc], kv_s.at[g, 0, 0])
        scores_of(g, y, True)
        return carry

    lax.fori_loop(0, 2, own_scores, 0)

    def all_weights(g, carry):
        def more_scores(t, inner):
            j = y - 1 - t
            for cc in range(2):
                arrived(kb.at[g, part(j * 2 + cc, 128, 128)], kv_r.at[g, 0, j * 2 + cc], kv_s.at[g, 0, 0])
            scores_of(g, j, False)
            return inner

        lax.fori_loop(0, y, more_scores, 0)
        row_max[g] = row_max[g] * LOG2_SCALE

        def weights_of(j, sums):
            rows = part(j, 256, 256)
            found = []
            for h in range(0, 8, 2):
                qs = slice(h * 256, h * 256 + 512)
                w = jnp.exp2(scores[g, rows, qs] * LOG2_SCALE - row_max[g, :, qs])
                scores[g, rows, qs] = w
                found.append(jnp.sum(w, axis=0, keepdims=True))
            return sums + jnp.concatenate(found, axis=1)

        sums = lax.fori_loop(0, y + 1, weights_of, jnp.zeros((1, 2048), F32))
        row_max[g] = 1.0 / sums
        dq_acc[g] = jnp.zeros((128, 2048), F32)
        return carry

    lax.fori_loop(0, 2, all_weights, 0)

    def grads_of(g, j):
        rows = part(j, 256, 256)
        keys, values = kb[g, rows, :], vb[g, rows, :]
        grad, query = heads_of(gb, g), heads_of(qb, g)
        prob_grad = dot(values, grad, 1, 1)
        prob = scores[g, rows, :] * row_max[g]
        score_grad = (prob * (prob_grad - delta_rows[g])).astype(BF)
        value_sum = dot(prob.astype(BF), grad, 1, 0)
        key_sum = dot(score_grad, query, 1, 0)
        dq_acc[g] = dq_acc[g] + dot(keys.T, score_grad, 1, 0)
        return key_sum * SCALE, value_sum

    def grads_copy(g, j):
        return remote(
            grads_out.at[g, j], grads_in.at[g, y], gr_s.at[g, j], gr_r.at[g, y], at(x, j, z, c)
        )

    def other_grads(g, carry):
        arrived(gb.at[other_rows, span_of(g)], sib_r.at[2 + g], sib_s.at[2 + g])
        arrived(deltas.at[4 + 2 * oc + g], sib_r.at[4 + g], sib_s.at[4 + g])
        arrived(vb.at[g, sib_rows], kv_r.at[g, 1, y * 2 + oc], kv_s.at[g, 1, 0])
        mine = deltas[2 * c + g]
        theirs = deltas[4 + 2 * oc + g]
        low_half = jnp.where(c == 0, mine, theirs)
        high_half = jnp.where(c == 0, theirs, mine)
        for h in range(8):
            delta_rows[g, :, h * 256:h * 256 + 128] = low_half[h:h + 1]
            delta_rows[g, :, h * 256 + 128:(h + 1) * 256] = high_half[h:h + 1]

        def far_grads(j, inner):
            for cc in range(2):
                arrived(vb.at[g, part(j * 2 + cc, 128, 128)], kv_r.at[g, 1, j * 2 + cc], kv_s.at[g, 1, 0])
            key_sum, value_sum = grads_of(g, j)
            grads_out[g, j, 0] = key_sum.astype(BF)
            grads_out[g, j, 1] = value_sum.astype(BF)
            grads_copy(g, j).start()
            return inner

        lax.fori_loop(0, y, far_grads, 0)
        return carry

    lax.fori_loop(0, 2, other_grads, 0)

    def last_grads(g, carry):
        key_sum, value_sum = grads_of(g, y)
        own_grads[g, 0] = key_sum
        own_grads[g, 1] = value_sum
        return carry

    lax.fori_loop(0, 2, last_grads, 0)
    for g in range(2):
        for h in range(8):
            first = (g * 8 + h) * 128
            dq_rows[:, first:first + 128] = (
                dq_acc[g, :, h * 256:(h + 1) * 256].T * SCALE
            ).astype(BF)

    arrived(down_act.at[other_rows], sib_r.at[6], sib_s.at[6])

    def put_tiles(term, first):
        for k in range(NY):
            for t in range(term.shape[1] // 128):
                up_part[k, first + t] = term[k * 16:(k + 1) * 16, t * 128:(t + 1) * 128]

    def send_group(e):
        tiles = pl.ds(e * 5, 5)
        for d in range(1, NY):
            yy = (y + d) % NY
            send(up_part.at[yy, tiles], up_y.at[y, tiles], uy_s.at[yy, e], uy_r.at[y, e],
                 at(x, yy, z, c))

    put_tiles(dot(down_act[:, 0:64], dq_rows[...], 0, 0).astype(BF), 0)
    for e in range(3):
        send_group(e)
    c_wq.wait()
    mid_part[:, 0:64] = dot(dq_rows[...], wq[...], 1, 1)

    c_wk.wait()
    c_wv.wait()
    for g in range(2):
        def add_later(yy, g=g):
            arrived(grads_in.at[g, yy], gr_r.at[g, yy], gr_s.at[g, 0])
            for which in range(2):
                own_grads[g, which] = own_grads[g, which] + grads_in[g, yy, which].astype(F32)

        each_later(add_later)
        for which in range(2):
            kv_rows[which, :, g * 128:(g + 1) * 128] = own_grads[g, which].astype(BF)
    for which in range(2):
        weight = (wk, wv)[which]
        mid_part[:, 64 + 64 * which:128 + 64 * which] = dot(kv_rows[which], weight[...], 1, 1)
    send(mid_part, mid_sib, sib_s.at[11], sib_r.at[11], sibling)
    for which in range(2):
        act = down_act[:, 64 + 64 * which:128 + 64 * which]
        put_tiles(dot(act, kv_rows[which], 0, 0).astype(BF), 16 + 2 * which)
    send_group(3)

    arrived(mid_sib, sib_r.at[11], sib_s.at[11])
    mid_all[part(x, 256, 256), :] = (mid_part[...] + mid_sib[...]).astype(BF)
    mid_rows = part(x * 2 + c, 128, 128)
    for d in range(1, NX):
        xx = (x + d) % NX
        send(mid_all.at[mid_rows], mid_all.at[mid_rows], mid_s.at[xx], mid_r.at[x], at(xx, y, z, c))

    for g in range(2):
        span = slice(g * 1024, (g + 1) * 1024)
        there = part(c * 2 + g, 1024, 1024)
        local(dq_rows.at[my_rows, span], dq_out.at[0, :, there], 14 + g)
        send(dq_rows.at[other_rows, span], dq_out.at[0, :, there], sib_s.at[7 + g], sib_r.at[7 + g], sibling)
    there = part(c, 256, 256)
    for which, out in ((0, dk_out), (1, dv_out)):
        local(kv_rows.at[which, my_rows], out.at[0, :, there], 16 + which)
        send(kv_rows.at[which, other_rows], out.at[0, :, there],
             sib_s.at[9 + which], sib_r.at[9 + which], sibling)

    def owner_of(k):
        return (k // 5) * NZ + k % 5

    def to_owner(k):
        return remote(
            up_sum.at[k], up_rs.at[dp], us_s.at[k], us_r.at[dp], {"dp": owner_of(k), "seq": seq}
        )

    def send_tile(k, carry):
        @pl.when(owner_of(k) != dp)
        def _():
            to_owner(k).start()
        return carry

    for e in range(4):
        tiles = pl.ds(e * 5, 5)
        up_y[y, tiles] = up_part[y, tiles]
        for d in range(1, NY):
            yy = (y + d) % NY
            arrived(up_y.at[yy, tiles], uy_r.at[yy, e], uy_s.at[0, 0])
        first, second = up_y[0, tiles].astype(F32), up_y[1, tiles].astype(F32)
        third, fourth = up_y[2, tiles].astype(F32), up_y[3, tiles].astype(F32)
        up_sum[tiles] = ((first + second) + (third + fourth)).astype(BF)
        lax.fori_loop(e * 5, e * 5 + 5, send_tile, 0)

    c_xc.wait()
    for d in range(1, NX):
        xx = (x + d) % NX
        rows = part(xx * 2 + c, 128, 128)
        arrived(mid_all.at[rows], mid_r.at[xx], mid_s.at[0])
        send(mid_all.at[rows], mid_all.at[rows], fwd_s.at[xx], fwd_r.at[xx], sibling)
    for d in range(NX):
        xx = (x + d) % NX
        for cc in ([oc] if d == 0 else [0, 1]):
            arrived(xcols.at[part(xx * 2 + cc, 128, 128)], x_r.at[xx * 2 + cc], x_s.at[0])
    for d in range(1, NX):
        xx = (x + d) % NX
        arrived(mid_all.at[part(xx * 2 + oc, 128, 128)], fwd_r.at[xx], fwd_s.at[0])
    mids = mid_all[...]
    for zz in range(4):
        found = dot(mids, xcols[:, zz * 256:(zz + 1) * 256], 0, 0).T
        for yy in range(NY):
            down_part[yy, zz] = found[yy * 64:(yy + 1) * 64, :].astype(BF)
        for d in range(1, NY):
            yy = (y + d) % NY
            send(down_part.at[yy, zz], down_y.at[y, zz], dy_s.at[yy, zz], dy_r.at[y, zz],
                 at(x, yy, z, c))

    own_tile = x * 5 + z
    owns = z < 5

    def final_copy(d):
        other = (dp + d) % (NX * NZ)
        return remote(
            up_fin.at[own_tile], up_fin.at[own_tile], ag_s.at[other], ag_r.at[own_tile],
            {"dp": other, "seq": seq},
        )

    @pl.when(owns)
    def _():
        up_rs[dp] = up_sum[own_tile]

        def wait_one(d, carry):
            other = (dp + d) % (NX * NZ)
            arrived(up_rs.at[other], us_r.at[other], us_s.at[0])
            return carry

        lax.fori_loop(1, NX * NZ, wait_one, 0)
        tile = jnp.sum(up_rs[...].astype(F32), axis=0)
        up_fin[own_tile] = (tile * FACTOR).astype(BF)

        def send_one(d, carry):
            final_copy(d).start()
            return carry

        lax.fori_loop(1, NX * NZ, send_one, 0)

    def down_copy(k, cc):
        return remote(
            down_z.at[k, cc * 32:(cc + 1) * 32], down_zin.at[z], dz_s.at[k, cc], dz_r.at[z],
            at(x, y, 4 * c + k, cc),
        )

    def wait_tile(k, carry):
        @pl.when(owner_of(k) != dp)
        def _():
            arrived(up_fin.at[k], ag_r.at[k], ag_s.at[0])
        return carry

    for k in range(4):
        down_y[y, k] = down_part[y, k]
        for d in range(1, NY):
            yy = (y + d) % NY
            arrived(down_y.at[yy, k], dy_r.at[yy, k], dy_s.at[0, 0])
        first, second = down_y[0, k].astype(F32), down_y[1, k].astype(F32)
        third, fourth = down_y[2, k].astype(F32), down_y[3, k].astype(F32)
        down_z[k] = ((first + second) + (third + fourth)).astype(BF)
        for cc in range(2):
            @pl.when(jnp.logical_or(4 * c + k != z, cc != c))
            def _():
                down_copy(k, cc).start()

        tiles = pl.ds(k * 5, 5)
        lax.fori_loop(k * 5, k * 5 + 5, wait_tile, 0)
        for d in range(1, NY):
            yy = (y + d) % NY
            send(up_fin.at[tiles], up_out.at[c, y, tiles], ay_s.at[yy, k], ay_r.at[y, k],
                 at(x, yy, z, c))
        local(up_fin.at[tiles], up_out.at[c, y, tiles], 18 + k)
        send(up_fin.at[tiles], up_out.at[c, y, tiles], sh_s.at[y, k], sh_r.at[y, k], sibling)

    source_core = z // 4

    @pl.when(source_core == c)
    def _():
        down_zin[z] = down_z[z % 4, part(c, 32, 32), :]

    for d in range(NZ):
        zz = (z + d) % NZ
        if d == 0:
            @pl.when(source_core != c)
            def _():
                arrived(down_zin.at[zz], dz_r.at[zz], dz_s.at[0, 0])
        else:
            arrived(down_zin.at[zz], dz_r.at[zz], dz_s.at[0, 0])
    down_out[...] = jnp.sum(down_zin[...].astype(F32), axis=0) * FACTOR

    for e in range(4):
        tiles = pl.ds(e * 5, 5)
        for d in range(1, NY):
            yy = (y + d) % NY
            arrived(up_out.at[c, yy, tiles], ay_r.at[yy, e], ay_s.at[0, 0])
            send(up_out.at[c, yy, tiles], up_out.at[c, yy, tiles], sh_s.at[yy, e], sh_r.at[yy, e],
                 sibling)

    for copy in locals_[14:]:
        copy.wait()
    for g in range(2):
        there = part(oc * 2 + g, 1024, 1024)
        arrived(dq_out.at[0, :, there], sib_r.at[7 + g], sib_s.at[7 + g])
    there = part(oc, 256, 256)
    arrived(dk_out.at[0, :, there], sib_r.at[9], sib_s.at[9])
    arrived(dv_out.at[0, :, there], sib_r.at[10], sib_s.at[10])
    for copy in started:
        copy.wait_send()
    for g in range(2):
        for which in range(2):
            def sent(yy, g=g, which=which):
                for cc in range(2):
                    kv_copy(g, which, yy, cc).wait_send()

            each_later(sent)

        def grads_sent(j, carry, g=g):
            grads_copy(g, j).wait_send()
            return carry

        lax.fori_loop(0, y, grads_sent, 0)

    def tile_sent(k, carry):
        @pl.when(owner_of(k) != dp)
        def _():
            to_owner(k).wait_send()
        return carry

    lax.fori_loop(0, 20, tile_sent, 0)

    @pl.when(owns)
    def _():
        def final_sent(d, carry):
            final_copy(d).wait_send()
            return carry

        lax.fori_loop(1, NX * NZ, final_sent, 0)

    for k in range(4):
        for cc in range(2):
            @pl.when(jnp.logical_or(4 * c + k != z, cc != c))
            def _():
                down_copy(k, cc).wait_send()
    for d in range(NY):
        yy = (y + d) % NY
        for e in range(4):
            arrived(up_out.at[oc, yy, pl.ds(e * 5, 5)], sh_r.at[yy, e], sh_s.at[0, 0])


def finish(
    dq_in, dk_in, dv_in, down_in, up_in, dq, dk, dv, down, upq, upk, upv,
    dq_v, dk_v, dv_v, up_v, upq_v, upk_v, upv_v, in_s, out_s,
):
    ins = [pltpu.make_async_copy(up_in, up_v, in_s.at[0])]
    outs = []
    for k in range(4):
        cols = pl.ds(k * 1024, 1024)
        ins.append(
            pltpu.make_async_copy(dq_in.at[:, :, cols], dq_v.at[:, :, cols], in_s.at[1 + k])
        )
        outs.append(pltpu.make_async_copy(dq_v.at[:, :, cols], dq.at[:, :, cols], out_s.at[k]))
    for k, (src, mid, dst) in enumerate(((dk_in, dk_v, dk), (dv_in, dv_v, dv))):
        ins.append(pltpu.make_async_copy(src, mid, in_s.at[5 + k]))
        outs.append(pltpu.make_async_copy(mid, dst, out_s.at[4 + k]))
    ups = [
        pltpu.make_async_copy(
            upq_v.at[pl.ds(k * 16, 16)], upq.at[pl.ds(k * 16, 16)], out_s.at[6 + k]
        )
        for k in range(NY)
    ]
    ups += [
        pltpu.make_async_copy(upk_v, upk, out_s.at[10]),
        pltpu.make_async_copy(upv_v, upv, out_s.at[11]),
    ]
    for copy in ins:
        copy.start()
    down[...] = down_in[...]
    for arriving, leaving in zip(ins[1:], outs):
        arriving.wait()
        leaving.start()
    ins[0].wait()
    for k in range(NY):
        rows = slice(k * 16, (k + 1) * 16)
        for cc in range(2):
            for t in range(20):
                tile = up_v[cc, k, t].astype(F32)
                if t < 16:
                    upq_v[rows, cc * 2048 + t * 128:cc * 2048 + (t + 1) * 128] = tile
                else:
                    first = cc * 256 + (t % 2) * 128
                    (upk_v if t < 18 else upv_v)[rows, first:first + 128] = tile
        ups[k].start()
    for copy in ups[4:]:
        copy.start()
    for copy in outs + ups:
        copy.wait()


def body(x_in, q_in, k_in, v_in, o_in, g_in, wd, wq, wk, wv):
    vm = pltpu.VMEM
    dma = pltpu.SemaphoreType.DMA
    any_ = pl.BlockSpec(memory_space=pl.ANY)
    vmem = pl.BlockSpec(memory_space=pltpu.VMEM)
    shape = jax.ShapeDtypeStruct
    scratch = [
        vm((128, 8192), BF), vm((192, 8192), BF), vm((64, 2048), BF), vm((64, 256), BF),
        vm((64, 256), BF), vm((256, 2048), BF), vm((256, 2048), BF), vm((2, 1024, 128), BF),
        vm((2, 1024, 128), BF), vm((128, 4096), BF), vm((128, 4096), BF), vm((8, 8, 128), F32),
        vm((256, 192), BF),
        vm((1024, 1024), BF), vm((2, 1024, 2048), F32), vm((2, 1, 2048), F32),
        vm((2, 1, 2048), F32),
        vm((2, 128, 2048), F32),
        vm((256, 2048), BF), vm((2, 4, 2, 256, 128), BF), vm((2, 4, 2, 256, 128), BF),
        vm((2, 2, 256, 128), F32),
        vm((2, 256, 256), BF), vm((256, 192), F32), vm((256, 192), F32), vm((1024, 192), BF),
        vm((4, 4, 64, 192), BF), vm((4, 4, 64, 192), BF), vm((4, 64, 192), BF), vm((8, 32, 192), BF),
        vm((4, 20, 16, 128), BF), vm((4, 20, 16, 128), BF), vm((20, 16, 128), BF),
        vm((32, 16, 128), BF), vm((20, 16, 128), BF),
        dma((22,)), dma((12,)), dma((12,)), dma((2, 2, 8)), dma((2, 2, 8)), dma((8,)), dma((8,)),
        dma((2, 4)), dma((2, 4)), dma((4,)), dma((4,)), dma((4,)), dma((4,)),
        dma((4, 4)), dma((4, 4)), dma((4, 2)), dma((8,)), dma((4, 4)), dma((4, 4)), dma((20,)), dma((32,)),
        dma((32,)), dma((20,)), dma((4, 4)), dma((4, 4)), dma((4, 4)), dma((4, 4)),
    ]
    first = pl.pallas_call(
        kernel,
        out_shape=[
            shape((1, 128, 4096), BF), shape((1, 128, 512), BF), shape((1, 128, 512), BF),
            shape((32, 192), F32), shape((2, 4, 20, 16, 128), BF),
        ],
        in_specs=[any_] * 10,
        out_specs=[any_] * 3 + [vmem, any_],
        scratch_shapes=scratch,
        compiler_params=pltpu.CompilerParams(
            vmem_limit_bytes=60 * 2**20, collective_id=0, has_side_effects=True
        ),
        cost_estimate=pl.CostEstimate(
            flops=8 * 10**9, bytes_accessed=12 * 2**20, transcendentals=4 * 2**20
        ),
    )(x_in, q_in, k_in, v_in, o_in, g_in, wd.T, wq, wk, wv)
    return pl.pallas_call(
        finish,
        out_shape=[
            shape((1, 128, 4096), BF), shape((1, 128, 512), BF), shape((1, 128, 512), BF),
            shape((32, 192), F32), shape((64, 4096), F32), shape((64, 512), F32),
            shape((64, 512), F32),
        ],
        in_specs=[any_] * 3 + [vmem, any_],
        out_specs=[any_] * 3 + [vmem] + [any_] * 3,
        scratch_shapes=[
            vm((1, 128, 4096), BF), vm((1, 128, 512), BF), vm((1, 128, 512), BF),
            vm((2, 4, 20, 16, 128), BF), vm((64, 4096), F32), vm((64, 512), F32),
            vm((64, 512), F32), dma((7,)), dma((12,)),
        ],
        compiler_params=pltpu.CompilerParams(vmem_limit_bytes=60 * 2**20),
        cost_estimate=pl.CostEstimate(flops=10**6, bytes_accessed=6 * 2**20, transcendentals=0),
    )(*first)


def solution(mesh):
    token = P("dp", "seq", None)
    return jax.shard_map(
        body,
        mesh=mesh,
        in_specs=(token,) * 6 + (P(),) * 4,
        out_specs=(token,) * 3 + (P(("dp", "seq"), None), P(), P(), P()),
        check_vma=False,
    )
```

time: 93 us -> 76.9 us (0.83)
  local copies, waits for them, and re-layouts: 12.6 us -> 0 us
  Pallas kernels: 79.5 us -> 76.1 us
    unnamed x20 -> x0, local copies, waits for them, and re-layouts: 12.6 us -> none
    pallas_call x1, Pallas kernels: 79.5 us -> 71.9 us  [body(): pl.pallas_call(kernel, out_shape=[shape((1, 128, 4096), BF), shape((1, 12...]
    pallas_call x0 -> x1, Pallas kernels: none -> 4.16 us  [body(): pl.pallas_call(finish, out_shape=[shape((1, 128, 4096), BF), shape((1, 12...]
where the time goes in v2:
time: 76.9 us; the launch traced here: 76.7 us
  Pallas kernels  76.1 us (99%)
    pallas_call x1, Pallas kernels, body(): pl.pallas_call(kernel, out_shape=[shape((1, 128, 4096), BF), shape((1, 12...  71.9 us
    pallas_call x1, Pallas kernels, body(): pl.pallas_call(finish, out_shape=[shape((1, 128, 4096), BF), shape((1, 12...  4.16 us

profile of v2, /device:TPU:1, one launch (start us, length us, event | category | flops | bytes accessed | tf_op | source)
XLA Modules:
  0.0 76.7 jit_solution(7921781164061592303)
XLA Ops:
  0.6 71.9 %shard_map.153 = (bf16[1,128,4096]{2,1,0:T(8,128)(2,1)}, bf16[1,128,512]{2,1,0:T(8,128)(2,1)}, bf16[1,128,512]{2,1,0:T(8,128)(2,1)}, f32[32,192]{1,0:T(8,128)}, bf16[2,4,20,16,128]{4,3,2,1,0:T(8,128)(2,1)}) custom-call(bf16[1,128,8192]{2,1,0:T(8,128)(2,1)} %x_in.1, bf16[1,128,4096]{2,1,0:T(8,128)(2,1)} %q_in.1, bf16[1,128,512]{2,1,0:T(8,128)(2,1)} %k_in.1, ...), custom_call_target="tpu_custom_call" | custom-call | flops 8000000000 | bytes 12582912 | tf_op jit(solution)/shard_map/pallas_call | solution.py:623
  72.6 4.2 %shard_map.154 = (bf16[1,128,4096]{2,1,0:T(8,128)(2,1)}, bf16[1,128,512]{2,1,0:T(8,128)(2,1)}, bf16[1,128,512]{2,1,0:T(8,128)(2,1)}, f32[32,192]{1,0:T(8,128)}, ...) custom-call(bf16[1,128,4096]{2,1,0:T(8,128)(2,1)} %get-tuple-element.12.dq_in, ...), custom_call_target="tpu_custom_call" | custom-call | flops 1000000 | bytes 6291456 | tf_op jit(solution)/shard_map/pallas_call | solution.py:639

commit v3 on v2

--- a/solution.py
+++ b/solution.py
@@ -50,8 +50,11 @@
             device_id=device, device_id_type=pl.DeviceIdType.MESH,
         )
 
-    def arrived(dst, rsem, ssem):
-        remote(dst, dst, ssem, rsem, sibling).wait_recv()
+    def arrived(dst, rsem):
+        remote(dst, dst, sib_s.at[0], rsem, sibling).wait_recv()
+
+    def left(src, ssem):
+        remote(src, src, ssem, sib_r.at[0], sibling).wait_send()
 
     def part(start, size, unit):
         return pl.ds(pl.multiple_of(start * unit, unit), size)
@@ -107,18 +110,19 @@
 
     started = []
 
-    def send(src, dst, ssem, rsem, device):
+    def send(src, dst, ssem, rsem, device, alone=False):
         copy = remote(src, dst, ssem, rsem, device)
         copy.start()
-        started.append(copy)
+        if alone:
+            started.append(copy)
 
     def kv_copy(g, which, yy, cc):
         source, target = ((k_in, kb), (v_in, vb))[which]
         return remote(
             source.at[0, :, part(2 * cc + g, 128, 128)],
             target.at[g, chip_rows],
-            kv_s.at[g, which, yy * 2 + cc],
-            kv_r.at[g, which, seq],
+            kv_s.at[yy],
+            kv_r.at[g, which, y],
             at(x, yy, z, cc),
         )
 
@@ -129,9 +133,7 @@
                 body(y + d)
 
     def send_kv(g, which):
-        copy = kv_copy(g, which, y, oc)
-        copy.start()
-        started.append(copy)
+        kv_copy(g, which, y, oc).start()
 
         def go(yy):
             for cc in range(2):
@@ -142,10 +144,13 @@
     def span_of(g):
         return part(g, 1024, 1024)
 
-    send_kv(0, 0)
     for g in range(2):
         send(q_in.at[0, :, span_of(oc * 2 + g)], qb.at[my_rows, span_of(g)],
-             sib_s.at[g], sib_r.at[g], sibling)
+             sib_s.at[g], sib_r.at[g], sibling, True)
+        for which in range(2):
+            send_kv(g, which)
+        send(g_in.at[0, :, span_of(oc * 2 + g)], gb.at[my_rows, span_of(g)],
+             sib_s.at[2 + g], sib_r.at[2 + g], sibling, True)
 
     c_gown.wait()
     c_oown.wait()
@@ -154,20 +159,14 @@
         == lax.broadcasted_iota(jnp.int32, (8, 1024), 0)
     ).astype(BF)
     for chunk in range(4):
-        if chunk == 2:
-            send_kv(1, 0)
         cols = slice(chunk * 1024, (chunk + 1) * 1024)
         product = gown[:, cols].astype(F32) * oown[:, cols].astype(F32)
         high = product.astype(BF)
         low = (product - high.astype(F32)).astype(BF)
         deltas[chunk] = dot(pick, high, 1, 1) + dot(pick, low, 1, 1)
     for g in range(2):
-        send(deltas.at[oc * 2 + g], deltas.at[4 + 2 * c + g], sib_s.at[4 + g], sib_r.at[4 + g], sibling)
-
-    send_kv(0, 1)
-    for g in range(2):
-        send(g_in.at[0, :, span_of(oc * 2 + g)], gb.at[my_rows, span_of(g)],
-             sib_s.at[2 + g], sib_r.at[2 + g], sibling)
+        send(deltas.at[oc * 2 + g], deltas.at[4 + 2 * c + g], sib_s.at[4 + g], sib_r.at[4 + g], sibling, True)
+
     c_x.wait()
     c_wd.wait()
     total = jnp.zeros((128, 192), F32)
@@ -175,14 +174,13 @@
         cols = slice(chunk * 2048, (chunk + 1) * 2048)
         total += dot(xv[:, cols], wd[:, cols], 1, 1)
     down_act[my_rows, :] = total.astype(BF)
-    send(down_act.at[my_rows], down_act.at[my_rows], sib_s.at[6], sib_r.at[6], sibling)
-    send_kv(1, 1)
+    send(down_act.at[my_rows], down_act.at[my_rows], sib_s.at[6], sib_r.at[6], sibling, True)
     for d in range(NX):
         for cc in ([oc] if d == 0 else [0, 1]):
             xx = (x + d) % NX
             send(x_in.at[0, :, part(xx * 2 + cc, 1024, 1024)],
                  xcols.at[part(x * 2 + c, 128, 128)],
-                 x_s.at[xx * 2 + cc], x_r.at[x * 2 + c], at(xx, y, z, cc))
+                 x_s.at[0], x_r.at[0], at(xx, y, z, cc))
 
     c_q.wait()
     c_g.wait()
@@ -210,18 +208,17 @@
         row_max[g] = top if first else jnp.maximum(row_max[g], top)
 
     def own_scores(g, carry):
-        arrived(qb.at[other_rows, span_of(g)], sib_r.at[g], sib_s.at[g])
-        arrived(kb.at[g, sib_rows], kv_r.at[g, 0, y * 2 + oc], kv_s.at[g, 0, 0])
+        arrived(qb.at[other_rows, span_of(g)], sib_r.at[g])
+        arrived(kb.at[g, sib_rows], kv_r.at[g, 0, y])
         scores_of(g, y, True)
         return carry
 
     lax.fori_loop(0, 2, own_scores, 0)
 
-    def all_weights(g, carry):
+    def all_weights(g):
         def more_scores(t, inner):
             j = y - 1 - t
-            for cc in range(2):
-                arrived(kb.at[g, part(j * 2 + cc, 128, 128)], kv_r.at[g, 0, j * 2 + cc], kv_s.at[g, 0, 0])
+            arrived(kb.at[g, part(j, 256, 256)], kv_r.at[g, 0, j])
             scores_of(g, j, False)
             return inner
 
@@ -241,9 +238,6 @@
         sums = lax.fori_loop(0, y + 1, weights_of, jnp.zeros((1, 2048), F32))
         row_max[g] = 1.0 / sums
         dq_acc[g] = jnp.zeros((128, 2048), F32)
-        return carry
-
-    lax.fori_loop(0, 2, all_weights, 0)
 
     def grads_of(g, j):
         rows = part(j, 256, 256)
@@ -259,13 +253,14 @@
 
     def grads_copy(g, j):
         return remote(
-            grads_out.at[g, j], grads_in.at[g, y], gr_s.at[g, j], gr_r.at[g, y], at(x, j, z, c)
+            grads_out.at[g, j], grads_in.at[g, y], gr_s.at[j], gr_r.at[y], at(x, j, z, c)
         )
 
     def other_grads(g, carry):
-        arrived(gb.at[other_rows, span_of(g)], sib_r.at[2 + g], sib_s.at[2 + g])
-        arrived(deltas.at[4 + 2 * oc + g], sib_r.at[4 + g], sib_s.at[4 + g])
-        arrived(vb.at[g, sib_rows], kv_r.at[g, 1, y * 2 + oc], kv_s.at[g, 1, 0])
+        all_weights(g)
+        arrived(gb.at[other_rows, span_of(g)], sib_r.at[2 + g])
+        arrived(deltas.at[4 + 2 * oc + g], sib_r.at[4 + g])
+        arrived(vb.at[g, sib_rows], kv_r.at[g, 1, y])
         mine = deltas[2 * c + g]
         theirs = deltas[4 + 2 * oc + g]
         low_half = jnp.where(c == 0, mine, theirs)
@@ -275,8 +270,7 @@
             delta_rows[g, :, h * 256 + 128:(h + 1) * 256] = high_half[h:h + 1]
 
         def far_grads(j, inner):
-            for cc in range(2):
-                arrived(vb.at[g, part(j * 2 + cc, 128, 128)], kv_r.at[g, 1, j * 2 + cc], kv_s.at[g, 1, 0])
+            arrived(vb.at[g, part(j, 256, 256)], kv_r.at[g, 1, j])
             key_sum, value_sum = grads_of(g, j)
             grads_out[g, j, 0] = key_sum.astype(BF)
             grads_out[g, j, 1] = value_sum.astype(BF)
@@ -302,7 +296,7 @@
                 dq_acc[g, :, h * 256:(h + 1) * 256].T * SCALE
             ).astype(BF)
 
-    arrived(down_act.at[other_rows], sib_r.at[6], sib_s.at[6])
+    arrived(down_act.at[other_rows], sib_r.at[6])
 
     def put_tiles(term, first):
         for k in range(NY):
@@ -313,7 +307,7 @@
         tiles = pl.ds(e * 5, 5)
         for d in range(1, NY):
             yy = (y + d) % NY
-            send(up_part.at[yy, tiles], up_y.at[y, tiles], uy_s.at[yy, e], uy_r.at[y, e],
+            send(up_part.at[yy, tiles], up_y.at[y, tiles], uy_s.at[0], uy_r.at[e],
                  at(x, yy, z, c))
 
     put_tiles(dot(down_act[:, 0:64], dq_rows[...], 0, 0).astype(BF), 0)
@@ -324,48 +318,49 @@
 
     c_wk.wait()
     c_wv.wait()
-    for g in range(2):
-        def add_later(yy, g=g):
-            arrived(grads_in.at[g, yy], gr_r.at[g, yy], gr_s.at[g, 0])
+    def add_later(yy):
+        arrived(grads_in.at[:, yy], gr_r.at[yy])
+        for g in range(2):
             for which in range(2):
                 own_grads[g, which] = own_grads[g, which] + grads_in[g, yy, which].astype(F32)
 
-        each_later(add_later)
+    each_later(add_later)
+    for g in range(2):
         for which in range(2):
             kv_rows[which, :, g * 128:(g + 1) * 128] = own_grads[g, which].astype(BF)
     for which in range(2):
         weight = (wk, wv)[which]
         mid_part[:, 64 + 64 * which:128 + 64 * which] = dot(kv_rows[which], weight[...], 1, 1)
-    send(mid_part, mid_sib, sib_s.at[11], sib_r.at[11], sibling)
+    send(mid_part, mid_sib, sib_s.at[11], sib_r.at[11], sibling, True)
     for which in range(2):
         act = down_act[:, 64 + 64 * which:128 + 64 * which]
         put_tiles(dot(act, kv_rows[which], 0, 0).astype(BF), 16 + 2 * which)
     send_group(3)
 
-    arrived(mid_sib, sib_r.at[11], sib_s.at[11])
+    arrived(mid_sib, sib_r.at[11])
     mid_all[part(x, 256, 256), :] = (mid_part[...] + mid_sib[...]).astype(BF)
     mid_rows = part(x * 2 + c, 128, 128)
     for d in range(1, NX):
         xx = (x + d) % NX
-        send(mid_all.at[mid_rows], mid_all.at[mid_rows], mid_s.at[xx], mid_r.at[x], at(xx, y, z, c))
+        send(mid_all.at[mid_rows], mid_all.at[mid_rows], mid_s.at[0], mid_r.at[x], at(xx, y, z, c))
 
     for g in range(2):
         span = slice(g * 1024, (g + 1) * 1024)
         there = part(c * 2 + g, 1024, 1024)
         local(dq_rows.at[my_rows, span], dq_out.at[0, :, there], 14 + g)
-        send(dq_rows.at[other_rows, span], dq_out.at[0, :, there], sib_s.at[7 + g], sib_r.at[7 + g], sibling)
+        send(dq_rows.at[other_rows, span], dq_out.at[0, :, there], sib_s.at[7 + g], sib_r.at[7 + g], sibling, True)
     there = part(c, 256, 256)
     for which, out in ((0, dk_out), (1, dv_out)):
         local(kv_rows.at[which, my_rows], out.at[0, :, there], 16 + which)
         send(kv_rows.at[which, other_rows], out.at[0, :, there],
-             sib_s.at[9 + which], sib_r.at[9 + which], sibling)
+             sib_s.at[9 + which], sib_r.at[9 + which], sibling, True)
 
     def owner_of(k):
         return (k // 5) * NZ + k % 5
 
     def to_owner(k):
         return remote(
-            up_sum.at[k], up_rs.at[dp], us_s.at[k], us_r.at[dp], {"dp": owner_of(k), "seq": seq}
+            up_sum.at[k], up_rs.at[dp], us_s.at[0], us_r.at[0], {"dp": owner_of(k), "seq": seq}
         )
 
     def send_tile(k, carry):
@@ -377,9 +372,7 @@
     for e in range(4):
         tiles = pl.ds(e * 5, 5)
         up_y[y, tiles] = up_part[y, tiles]
-        for d in range(1, NY):
-            yy = (y + d) % NY
-            arrived(up_y.at[yy, tiles], uy_r.at[yy, e], uy_s.at[0, 0])
+        arrived(up_y.at[0:NY - 1, tiles], uy_r.at[e])
         first, second = up_y[0, tiles].astype(F32), up_y[1, tiles].astype(F32)
         third, fourth = up_y[2, tiles].astype(F32), up_y[3, tiles].astype(F32)
         up_sum[tiles] = ((first + second) + (third + fourth)).astype(BF)
@@ -389,15 +382,10 @@
     for d in range(1, NX):
         xx = (x + d) % NX
         rows = part(xx * 2 + c, 128, 128)
-        arrived(mid_all.at[rows], mid_r.at[xx], mid_s.at[0])
-        send(mid_all.at[rows], mid_all.at[rows], fwd_s.at[xx], fwd_r.at[xx], sibling)
-    for d in range(NX):
-        xx = (x + d) % NX
-        for cc in ([oc] if d == 0 else [0, 1]):
-            arrived(xcols.at[part(xx * 2 + cc, 128, 128)], x_r.at[xx * 2 + cc], x_s.at[0])
-    for d in range(1, NX):
-        xx = (x + d) % NX
-        arrived(mid_all.at[part(xx * 2 + oc, 128, 128)], fwd_r.at[xx], fwd_s.at[0])
+        arrived(mid_all.at[rows], mid_r.at[xx])
+        send(mid_all.at[rows], mid_all.at[rows], fwd_s.at[0], fwd_r.at[0], sibling)
+    arrived(xcols.at[0:128 * (2 * NX - 1)], x_r.at[0])
+    arrived(mid_all.at[0:128 * (NX - 1)], fwd_r.at[0])
     mids = mid_all[...]
     for zz in range(4):
         found = dot(mids, xcols[:, zz * 256:(zz + 1) * 256], 0, 0).T
@@ -405,7 +393,7 @@
             down_part[yy, zz] = found[yy * 64:(yy + 1) * 64, :].astype(BF)
         for d in range(1, NY):
             yy = (y + d) % NY
-            send(down_part.at[yy, zz], down_y.at[y, zz], dy_s.at[yy, zz], dy_r.at[y, zz],
+            send(down_part.at[yy, zz], down_y.at[y, zz], dy_s.at[0], dy_r.at[zz],
                  at(x, yy, z, c))
 
     own_tile = x * 5 + z
@@ -414,7 +402,7 @@
     def final_copy(d):
         other = (dp + d) % (NX * NZ)
         return remote(
-            up_fin.at[own_tile], up_fin.at[own_tile], ag_s.at[other], ag_r.at[own_tile],
+            up_fin.at[own_tile], up_fin.at[own_tile], ag_s.at[0], ag_r.at[x],
             {"dp": other, "seq": seq},
         )
 
@@ -422,12 +410,7 @@
     def _():
         up_rs[dp] = up_sum[own_tile]
 
-        def wait_one(d, carry):
-            other = (dp + d) % (NX * NZ)
-            arrived(up_rs.at[other], us_r.at[other], us_s.at[0])
-            return carry
-
-        lax.fori_loop(1, NX * NZ, wait_one, 0)
+        arrived(up_rs.at[0:NX * NZ - 1], us_r.at[0])
         tile = jnp.sum(up_rs[...].astype(F32), axis=0)
         up_fin[own_tile] = (tile * FACTOR).astype(BF)
 
@@ -439,21 +422,13 @@
 
     def down_copy(k, cc):
         return remote(
-            down_z.at[k, cc * 32:(cc + 1) * 32], down_zin.at[z], dz_s.at[k, cc], dz_r.at[z],
+            down_z.at[k, cc * 32:(cc + 1) * 32], down_zin.at[z], dz_s.at[0], dz_r.at[0],
             at(x, y, 4 * c + k, cc),
         )
-
-    def wait_tile(k, carry):
-        @pl.when(owner_of(k) != dp)
-        def _():
-            arrived(up_fin.at[k], ag_r.at[k], ag_s.at[0])
-        return carry
 
     for k in range(4):
         down_y[y, k] = down_part[y, k]
-        for d in range(1, NY):
-            yy = (y + d) % NY
-            arrived(down_y.at[yy, k], dy_r.at[yy, k], dy_s.at[0, 0])
+        arrived(down_y.at[0:NY - 1, k], dy_r.at[k])
         first, second = down_y[0, k].astype(F32), down_y[1, k].astype(F32)
         third, fourth = down_y[2, k].astype(F32), down_y[3, k].astype(F32)
         down_z[k] = ((first + second) + (third + fourth)).astype(BF)
@@ -463,13 +438,22 @@
                 down_copy(k, cc).start()
 
         tiles = pl.ds(k * 5, 5)
-        lax.fori_loop(k * 5, k * 5 + 5, wait_tile, 0)
+        mine = jnp.logical_and(x == k, owns)
+
+        @pl.when(mine)
+        def _():
+            arrived(up_fin.at[0:4], ag_r.at[k])
+
+        @pl.when(jnp.logical_not(mine))
+        def _():
+            arrived(up_fin.at[0:5], ag_r.at[k])
+
         for d in range(1, NY):
             yy = (y + d) % NY
-            send(up_fin.at[tiles], up_out.at[c, y, tiles], ay_s.at[yy, k], ay_r.at[y, k],
+            send(up_fin.at[tiles], up_out.at[c, y, tiles], ay_s.at[0], ay_r.at[k],
                  at(x, yy, z, c))
         local(up_fin.at[tiles], up_out.at[c, y, tiles], 18 + k)
-        send(up_fin.at[tiles], up_out.at[c, y, tiles], sh_s.at[y, k], sh_r.at[y, k], sibling)
+        send(up_fin.at[tiles], up_out.at[c, y, tiles], sh_s.at[0], sh_r.at[0], sibling)
 
     source_core = z // 4
 
@@ -477,73 +461,71 @@
     def _():
         down_zin[z] = down_z[z % 4, part(c, 32, 32), :]
 
-    for d in range(NZ):
-        zz = (z + d) % NZ
-        if d == 0:
-            @pl.when(source_core != c)
-            def _():
-                arrived(down_zin.at[zz], dz_r.at[zz], dz_s.at[0, 0])
-        else:
-            arrived(down_zin.at[zz], dz_r.at[zz], dz_s.at[0, 0])
+    @pl.when(source_core == c)
+    def _():
+        arrived(down_zin.at[0:NZ - 1], dz_r.at[0])
+
+    @pl.when(source_core != c)
+    def _():
+        arrived(down_zin, dz_r.at[0])
+
     down_out[...] = jnp.sum(down_zin[...].astype(F32), axis=0) * FACTOR
 
     for e in range(4):
         tiles = pl.ds(e * 5, 5)
+        arrived(up_out.at[c, 0:NY - 1, tiles], ay_r.at[e])
         for d in range(1, NY):
             yy = (y + d) % NY
-            arrived(up_out.at[c, yy, tiles], ay_r.at[yy, e], ay_s.at[0, 0])
-            send(up_out.at[c, yy, tiles], up_out.at[c, yy, tiles], sh_s.at[yy, e], sh_r.at[yy, e],
-                 sibling)
+            send(up_out.at[c, yy, tiles], up_out.at[c, yy, tiles], sh_s.at[0], sh_r.at[0], sibling)
 
     for copy in locals_[14:]:
         copy.wait()
     for g in range(2):
         there = part(oc * 2 + g, 1024, 1024)
-        arrived(dq_out.at[0, :, there], sib_r.at[7 + g], sib_s.at[7 + g])
+        arrived(dq_out.at[0, :, there], sib_r.at[7 + g])
     there = part(oc, 256, 256)
-    arrived(dk_out.at[0, :, there], sib_r.at[9], sib_s.at[9])
-    arrived(dv_out.at[0, :, there], sib_r.at[10], sib_s.at[10])
+    arrived(dk_out.at[0, :, there], sib_r.at[9])
+    arrived(dv_out.at[0, :, there], sib_r.at[10])
     for copy in started:
         copy.wait_send()
-    for g in range(2):
-        for which in range(2):
-            def sent(yy, g=g, which=which):
-                for cc in range(2):
-                    kv_copy(g, which, yy, cc).wait_send()
-
-            each_later(sent)
-
-        def grads_sent(j, carry, g=g):
-            grads_copy(g, j).wait_send()
-            return carry
-
-        lax.fori_loop(0, y, grads_sent, 0)
-
-    def tile_sent(k, carry):
-        @pl.when(owner_of(k) != dp)
-        def _():
-            to_owner(k).wait_send()
+    left(kb.at[:, 0:256], kv_s.at[y])
+
+    def sent_later(yy):
+        left(kb.at[:, 0:512], kv_s.at[yy])
+
+    each_later(sent_later)
+
+    def grads_sent(j, carry):
+        left(grads_out.at[:, j], gr_s.at[j])
         return carry
 
-    lax.fori_loop(0, 20, tile_sent, 0)
+    lax.fori_loop(0, y, grads_sent, 0)
+    left(xcols.at[0:128 * (2 * NX - 1)], x_s.at[0])
+    left(mid_all.at[0:128 * (NX - 1)], mid_s.at[0])
+    left(mid_all.at[0:128 * (NX - 1)], fwd_s.at[0])
+    left(down_part.at[0:NY - 1], dy_s.at[0])
+    left(up_part.at[0:NY - 1], uy_s.at[0])
+    left(up_out.at[c, 0:NY - 1], ay_s.at[0])
+    left(up_out.at[c], sh_s.at[0])
 
     @pl.when(owns)
     def _():
-        def final_sent(d, carry):
-            final_copy(d).wait_send()
-            return carry
-
-        lax.fori_loop(1, NX * NZ, final_sent, 0)
-
-    for k in range(4):
-        for cc in range(2):
-            @pl.when(jnp.logical_or(4 * c + k != z, cc != c))
-            def _():
-                down_copy(k, cc).wait_send()
-    for d in range(NY):
-        yy = (y + d) % NY
-        for e in range(4):
-            arrived(up_out.at[oc, yy, pl.ds(e * 5, 5)], sh_r.at[yy, e], sh_s.at[0, 0])
+        left(up_sum.at[0:19], us_s.at[0])
+        left(up_rs.at[0:NX * NZ - 1], ag_s.at[0])
+
+    @pl.when(jnp.logical_not(owns))
+    def _():
+        left(up_sum, us_s.at[0])
+
+    @pl.when(source_core == c)
+    def _():
+        left(down_zin.at[0:NZ - 1], dz_s.at[0])
+
+    @pl.when(source_core != c)
+    def _():
+        left(down_zin, dz_s.at[0])
+
+    arrived(up_out.at[oc], sh_r.at[0])
 
 
 def finish(
@@ -615,10 +597,10 @@
         vm((4, 4, 64, 192), BF), vm((4, 4, 64, 192), BF), vm((4, 64, 192), BF), vm((8, 32, 192), BF),
         vm((4, 20, 16, 128), BF), vm((4, 20, 16, 128), BF), vm((20, 16, 128), BF),
         vm((32, 16, 128), BF), vm((20, 16, 128), BF),
-        dma((22,)), dma((12,)), dma((12,)), dma((2, 2, 8)), dma((2, 2, 8)), dma((8,)), dma((8,)),
-        dma((2, 4)), dma((2, 4)), dma((4,)), dma((4,)), dma((4,)), dma((4,)),
-        dma((4, 4)), dma((4, 4)), dma((4, 2)), dma((8,)), dma((4, 4)), dma((4, 4)), dma((20,)), dma((32,)),
-        dma((32,)), dma((20,)), dma((4, 4)), dma((4, 4)), dma((4, 4)), dma((4, 4)),
+        dma((22,)), dma((12,)), dma((12,)), dma((4,)), dma((2, 2, 4)), dma((1,)), dma((1,)),
+        dma((4,)), dma((4,)), dma((1,)), dma((4,)), dma((1,)), dma((1,)),
+        dma((1,)), dma((4,)), dma((1,)), dma((1,)), dma((1,)), dma((4,)), dma((1,)), dma((1,)),
+        dma((1,)), dma((4,)), dma((1,)), dma((4,)), dma((1,)), dma((1,)),
     ]
     first = pl.pallas_call(
         kernel,

time: 76.9 us -> 71.3 us (0.927)
  Pallas kernels: 76.1 us -> 70.5 us
    pallas_call x1, Pallas kernels: 71.9 us -> 66.3 us  [body(): pl.pallas_call(kernel, out_shape=[shape((1, 128, 4096), BF), shape((1, 12...]
where the time goes in v3:
time: 71.3 us; the launch traced here: 71.1 us
  Pallas kernels  70.5 us (99%)
    pallas_call x1, Pallas kernels, body(): pl.pallas_call(kernel, out_shape=[shape((1, 128, 4096), BF), shape((1, 12...  66.3 us
    pallas_call x1, Pallas kernels, body(): pl.pallas_call(finish, out_shape=[shape((1, 128, 4096), BF), shape((1, 12...  4.16 us

profile of v3, /device:TPU:1, one launch (start us, length us, event | category | flops | bytes accessed | tf_op | source)
XLA Modules:
  0.0 71.1 jit_solution(2244420912136542042)
XLA Ops:
  0.6 66.3 %shard_map.153 = (bf16[1,128,4096]{2,1,0:T(8,128)(2,1)}, bf16[1,128,512]{2,1,0:T(8,128)(2,1)}, bf16[1,128,512]{2,1,0:T(8,128)(2,1)}, f32[32,192]{1,0:T(8,128)}, bf16[2,4,20,16,128]{4,3,2,1,0:T(8,128)(2,1)}) custom-call(bf16[1,128,8192]{2,1,0:T(8,128)(2,1)} %x_in.1, bf16[1,128,4096]{2,1,0:T(8,128)(2,1)} %q_in.1, bf16[1,128,512]{2,1,0:T(8,128)(2,1)} %k_in.1, ...), custom_call_target="tpu_custom_call" | custom-call | flops 8000000000 | bytes 12582912 | tf_op jit(solution)/shard_map/pallas_call | solution.py:605
  67.0 4.2 %shard_map.154 = (bf16[1,128,4096]{2,1,0:T(8,128)(2,1)}, bf16[1,128,512]{2,1,0:T(8,128)(2,1)}, bf16[1,128,512]{2,1,0:T(8,128)(2,1)}, f32[32,192]{1,0:T(8,128)}, ...) custom-call(bf16[1,128,4096]{2,1,0:T(8,128)(2,1)} %get-tuple-element.12.dq_in, ...), custom_call_target="tpu_custom_call" | custom-call | flops 1000000 | bytes 6291456 | tf_op jit(solution)/shard_map/pallas_call | solution.py:621

commit v4 on v3

--- a/solution.py
+++ b/solution.py
@@ -28,7 +28,7 @@
     dq_out, dk_out, dv_out, down_out, up_out,
     xv, wd, wq, wk, wv, qb, gb, kb, vb, gown, oown, deltas, down_act,
     xcols, scores, row_max, delta_rows, dq_acc, dq_rows, grads_out, grads_in, own_grads,
-    kv_rows, mid_part, mid_sib, mid_all, down_part, down_y, down_z, down_zin,
+    kv_rows, mid_part, mid_sib, mid_all, down_part, down_y, down_z, down_zin, down_sum,
     up_part, up_y, up_sum, up_rs, up_fin,
     loc, sib_s, sib_r, kv_s, kv_r, x_s, x_r, gr_s, gr_r, mid_s, mid_r, fwd_s, fwd_r,
     dy_s, dy_r, dz_s, dz_r, uy_s, uy_r, us_s, us_r, ag_s, ag_r, ay_s, ay_r, sh_s, sh_r,
@@ -127,10 +127,10 @@
         )
 
     def each_later(body):
-        for d in range(1, NY):
-            @pl.when(y + d < NY)
+        for yy in range(NY - 1, 0, -1):
+            @pl.when(y < yy)
             def _():
-                body(y + d)
+                body(yy)
 
     def send_kv(g, which):
         kv_copy(g, which, y, oc).start()
@@ -378,6 +378,30 @@
         up_sum[tiles] = ((first + second) + (third + fourth)).astype(BF)
         lax.fori_loop(e * 5, e * 5 + 5, send_tile, 0)
 
+    own_tile = x * 5 + z
+    owns = z < 5
+
+    def final_copy(d):
+        other = (dp + d) % (NX * NZ)
+        return remote(
+            up_fin.at[own_tile], up_fin.at[own_tile], ag_s.at[0], ag_r.at[x],
+            {"dp": other, "seq": seq},
+        )
+
+    @pl.when(owns)
+    def _():
+        up_rs[dp] = up_sum[own_tile]
+
+        arrived(up_rs.at[0:NX * NZ - 1], us_r.at[0])
+        tile = jnp.sum(up_rs[...].astype(F32), axis=0)
+        up_fin[own_tile] = (tile * FACTOR).astype(BF)
+
+        def send_one(d, carry):
+            final_copy(d).start()
+            return carry
+
+        lax.fori_loop(1, NX * NZ, send_one, 0)
+
     c_xc.wait()
     for d in range(1, NX):
         xx = (x + d) % NX
@@ -387,38 +411,18 @@
     arrived(xcols.at[0:128 * (2 * NX - 1)], x_r.at[0])
     arrived(mid_all.at[0:128 * (NX - 1)], fwd_r.at[0])
     mids = mid_all[...]
-    for zz in range(4):
-        found = dot(mids, xcols[:, zz * 256:(zz + 1) * 256], 0, 0).T
+    for p in range(2):
+        blocks = [
+            dot(mids, xcols[:, zz * 256:(zz + 1) * 256], 0, 0) for zz in (2 * p, 2 * p + 1)
+        ]
+        packed = [found[0:128].T for found in blocks]
+        packed.append(jnp.concatenate([found[128:192] for found in blocks], axis=0).T)
         for yy in range(NY):
-            down_part[yy, zz] = found[yy * 64:(yy + 1) * 64, :].astype(BF)
+            for k in range(3):
+                down_part[yy, p, k] = packed[k][yy * 64:(yy + 1) * 64, :].astype(BF)
         for d in range(1, NY):
             yy = (y + d) % NY
-            send(down_part.at[yy, zz], down_y.at[y, zz], dy_s.at[0], dy_r.at[zz],
-                 at(x, yy, z, c))
-
-    own_tile = x * 5 + z
-    owns = z < 5
-
-    def final_copy(d):
-        other = (dp + d) % (NX * NZ)
-        return remote(
-            up_fin.at[own_tile], up_fin.at[own_tile], ag_s.at[0], ag_r.at[x],
-            {"dp": other, "seq": seq},
-        )
-
-    @pl.when(owns)
-    def _():
-        up_rs[dp] = up_sum[own_tile]
-
-        arrived(up_rs.at[0:NX * NZ - 1], us_r.at[0])
-        tile = jnp.sum(up_rs[...].astype(F32), axis=0)
-        up_fin[own_tile] = (tile * FACTOR).astype(BF)
-
-        def send_one(d, carry):
-            final_copy(d).start()
-            return carry
-
-        lax.fori_loop(1, NX * NZ, send_one, 0)
+            send(down_part.at[yy, p], down_y.at[y, p], dy_s.at[0], dy_r.at[p], at(x, yy, z, c))
 
     def down_copy(k, cc):
         return remote(
@@ -427,11 +431,17 @@
         )
 
     for k in range(4):
-        down_y[y, k] = down_part[y, k]
-        arrived(down_y.at[0:NY - 1, k], dy_r.at[k])
-        first, second = down_y[0, k].astype(F32), down_y[1, k].astype(F32)
-        third, fourth = down_y[2, k].astype(F32), down_y[3, k].astype(F32)
-        down_z[k] = ((first + second) + (third + fourth)).astype(BF)
+        if k % 2 == 0:
+            p = k // 2
+            down_y[y, p] = down_part[y, p]
+            arrived(down_y.at[0:NY - 1, p], dy_r.at[p])
+            first, second = down_y[0, p].astype(F32), down_y[1, p].astype(F32)
+            third, fourth = down_y[2, p].astype(F32), down_y[3, p].astype(F32)
+            summed = (first + second) + (third + fourth)
+            for i in range(2):
+                down_z[k + i] = jnp.concatenate(
+                    [summed[i], summed[2][:, i * 64:(i + 1) * 64]], axis=1
+                ).astype(BF)
         for cc in range(2):
             @pl.when(jnp.logical_or(4 * c + k != z, cc != c))
             def _():
@@ -469,7 +479,8 @@
     def _():
         arrived(down_zin, dz_r.at[0])
 
-    down_out[...] = jnp.sum(down_zin[...].astype(F32), axis=0) * FACTOR
+    down_sum[...] = jnp.sum(down_zin[...].astype(F32), axis=0) * FACTOR
+    local(down_sum, down_out, 22)
 
     for e in range(4):
         tiles = pl.ds(e * 5, 5)
@@ -530,7 +541,7 @@
 
 def finish(
     dq_in, dk_in, dv_in, down_in, up_in, dq, dk, dv, down, upq, upk, upv,
-    dq_v, dk_v, dv_v, up_v, upq_v, upk_v, upv_v, in_s, out_s,
+    dq_v, dk_v, dv_v, down_v, up_v, upq_v, upk_v, upv_v, in_s, out_s,
 ):
     ins = [pltpu.make_async_copy(up_in, up_v, in_s.at[0])]
     outs = []
@@ -540,22 +551,23 @@
             pltpu.make_async_copy(dq_in.at[:, :, cols], dq_v.at[:, :, cols], in_s.at[1 + k])
         )
         outs.append(pltpu.make_async_copy(dq_v.at[:, :, cols], dq.at[:, :, cols], out_s.at[k]))
-    for k, (src, mid, dst) in enumerate(((dk_in, dk_v, dk), (dv_in, dv_v, dv))):
+    for k, (src, mid, dst) in enumerate(
+        ((dk_in, dk_v, dk), (dv_in, dv_v, dv), (down_in, down_v, down))
+    ):
         ins.append(pltpu.make_async_copy(src, mid, in_s.at[5 + k]))
         outs.append(pltpu.make_async_copy(mid, dst, out_s.at[4 + k]))
     ups = [
         pltpu.make_async_copy(
-            upq_v.at[pl.ds(k * 16, 16)], upq.at[pl.ds(k * 16, 16)], out_s.at[6 + k]
+            upq_v.at[pl.ds(k * 16, 16)], upq.at[pl.ds(k * 16, 16)], out_s.at[7 + k]
         )
         for k in range(NY)
     ]
     ups += [
-        pltpu.make_async_copy(upk_v, upk, out_s.at[10]),
-        pltpu.make_async_copy(upv_v, upv, out_s.at[11]),
+        pltpu.make_async_copy(upk_v, upk, out_s.at[11]),
+        pltpu.make_async_copy(upv_v, upv, out_s.at[12]),
     ]
     for copy in ins:
         copy.start()
-    down[...] = down_in[...]
     for arriving, leaving in zip(ins[1:], outs):
         arriving.wait()
         leaving.start()
@@ -581,7 +593,6 @@
     vm = pltpu.VMEM
     dma = pltpu.SemaphoreType.DMA
     any_ = pl.BlockSpec(memory_space=pl.ANY)
-    vmem = pl.BlockSpec(memory_space=pltpu.VMEM)
     shape = jax.ShapeDtypeStruct
     scratch = [
         vm((128, 8192), BF), vm((192, 8192), BF), vm((64, 2048), BF), vm((64, 256), BF),
@@ -594,10 +605,11 @@
         vm((256, 2048), BF), vm((2, 4, 2, 256, 128), BF), vm((2, 4, 2, 256, 128), BF),
         vm((2, 2, 256, 128), F32),
         vm((2, 256, 256), BF), vm((256, 192), F32), vm((256, 192), F32), vm((1024, 192), BF),
-        vm((4, 4, 64, 192), BF), vm((4, 4, 64, 192), BF), vm((4, 64, 192), BF), vm((8, 32, 192), BF),
+        vm((4, 2, 3, 64, 128), BF), vm((4, 2, 3, 64, 128), BF), vm((4, 64, 192), BF), vm((8, 32, 192), BF),
+        vm((32, 192), F32),
         vm((4, 20, 16, 128), BF), vm((4, 20, 16, 128), BF), vm((20, 16, 128), BF),
         vm((32, 16, 128), BF), vm((20, 16, 128), BF),
-        dma((22,)), dma((12,)), dma((12,)), dma((4,)), dma((2, 2, 4)), dma((1,)), dma((1,)),
+        dma((23,)), dma((12,)), dma((12,)), dma((4,)), dma((2, 2, 4)), dma((1,)), dma((1,)),
         dma((4,)), dma((4,)), dma((1,)), dma((4,)), dma((1,)), dma((1,)),
         dma((1,)), dma((4,)), dma((1,)), dma((1,)), dma((1,)), dma((4,)), dma((1,)), dma((1,)),
         dma((1,)), dma((4,)), dma((1,)), dma((4,)), dma((1,)), dma((1,)),
@@ -609,7 +621,7 @@
             shape((32, 192), F32), shape((2, 4, 20, 16, 128), BF),
         ],
         in_specs=[any_] * 10,
-        out_specs=[any_] * 3 + [vmem, any_],
+        out_specs=[any_] * 5,
         scratch_shapes=scratch,
         compiler_params=pltpu.CompilerParams(
             vmem_limit_bytes=60 * 2**20, collective_id=0, has_side_effects=True
@@ -625,12 +637,12 @@
             shape((32, 192), F32), shape((64, 4096), F32), shape((64, 512), F32),
             shape((64, 512), F32),
         ],
-        in_specs=[any_] * 3 + [vmem, any_],
-        out_specs=[any_] * 3 + [vmem] + [any_] * 3,
+        in_specs=[any_] * 5,
+        out_specs=[any_] * 7,
         scratch_shapes=[
             vm((1, 128, 4096), BF), vm((1, 128, 512), BF), vm((1, 128, 512), BF),
-            vm((2, 4, 20, 16, 128), BF), vm((64, 4096), F32), vm((64, 512), F32),
-            vm((64, 512), F32), dma((7,)), dma((12,)),
+            vm((32, 192), F32), vm((2, 4, 20, 16, 128), BF), vm((64, 4096), F32),
+            vm((64, 512), F32), vm((64, 512), F32), dma((8,)), dma((13,)),
         ],
         compiler_params=pltpu.CompilerParams(vmem_limit_bytes=60 * 2**20),
         cost_estimate=pl.CostEstimate(flops=10**6, bytes_accessed=6 * 2**20, transcendentals=0),

time: 71.3 us -> 67.6 us (0.948)
  Pallas kernels: 70.5 us -> 66.8 us
    pallas_call x1, Pallas kernels: 66.3 us -> 64 us  [body(): pl.pallas_call(kernel, out_shape=[shape((1, 128, 4096), BF), shape((1, 12...]
    pallas_call x1, Pallas kernels: 4.16 us -> 2.82 us  [body(): pl.pallas_call(finish, out_shape=[shape((1, 128, 4096), BF), shape((1, 12...]
where the time goes in v4:
time: 67.6 us; the launch traced here: 67.5 us
  Pallas kernels  66.8 us (99%)
    pallas_call x1, Pallas kernels, body(): pl.pallas_call(kernel, out_shape=[shape((1, 128, 4096), BF), shape((1, 12...  64 us
    pallas_call x1, Pallas kernels, body(): pl.pallas_call(finish, out_shape=[shape((1, 128, 4096), BF), shape((1, 12...  2.82 us

profile of v4, /device:TPU:1, one launch (start us, length us, event | category | flops | bytes accessed | tf_op | source)
XLA Modules:
  0.0 67.5 jit_solution(7189503372481296182)
XLA Ops:
  0.6 64.0 %shard_map.153 = (bf16[1,128,4096]{2,1,0:T(8,128)(2,1)}, bf16[1,128,512]{2,1,0:T(8,128)(2,1)}, bf16[1,128,512]{2,1,0:T(8,128)(2,1)}, f32[32,192]{1,0:T(8,128)}, bf16[2,4,20,16,128]{4,3,2,1,0:T(8,128)(2,1)}) custom-call(bf16[1,128,8192]{2,1,0:T(8,128)(2,1)} %x_in.1, bf16[1,128,4096]{2,1,0:T(8,128)(2,1)} %q_in.1, bf16[1,128,512]{2,1,0:T(8,128)(2,1)} %k_in.1, ...), custom_call_target="tpu_custom_call" | custom-call | flops 8000000000 | bytes 12582912 | tf_op jit(solution)/shard_map/pallas_call | solution.py:617
  64.7 2.8 %shard_map.154 = (bf16[1,128,4096]{2,1,0:T(8,128)(2,1)}, bf16[1,128,512]{2,1,0:T(8,128)(2,1)}, bf16[1,128,512]{2,1,0:T(8,128)(2,1)}, f32[32,192]{1,0:T(8,128)}, ...) custom-call(bf16[1,128,4096]{2,1,0:T(8,128)(2,1)} %get-tuple-element.12.dq_in, ...), custom_call_target="tpu_custom_call" | custom-call | flops 1000000 | bytes 6291456 | tf_op jit(solution)/shard_map/pallas_call | solution.py:633

commit v5 on v4

--- a/solution.py
+++ b/solution.py
@@ -269,7 +269,8 @@
             delta_rows[g, :, h * 256:h * 256 + 128] = low_half[h:h + 1]
             delta_rows[g, :, h * 256 + 128:(h + 1) * 256] = high_half[h:h + 1]
 
-        def far_grads(j, inner):
+        def far_grads(t, inner):
+            j = jnp.where(t == 0, jnp.maximum(y - 2, 0), jnp.where(t == y - 1, y - 1, t - 1))
             arrived(vb.at[g, part(j, 256, 256)], kv_r.at[g, 1, j])
             key_sum, value_sum = grads_of(g, j)
             grads_out[g, j, 0] = key_sum.astype(BF)
@@ -431,6 +432,25 @@
         )
 
     for k in range(4):
+        tiles = pl.ds(k * 5, 5)
+        mine = jnp.logical_and(x == k, owns)
+
+        @pl.when(mine)
+        def _():
+            arrived(up_fin.at[0:4], ag_r.at[k])
+
+        @pl.when(jnp.logical_not(mine))
+        def _():
+            arrived(up_fin.at[0:5], ag_r.at[k])
+
+        for d in range(1, NY):
+            yy = (y + d) % NY
+            send(up_fin.at[tiles], up_out.at[c, y, tiles], ay_s.at[0], ay_r.at[k],
+                 at(x, yy, z, c))
+        local(up_fin.at[tiles], up_out.at[c, y, tiles], 18 + k)
+        send(up_fin.at[tiles], up_out.at[c, y, tiles], sh_s.at[0], sh_r.at[0], sibling)
+
+    for k in range(4):
         if k % 2 == 0:
             p = k // 2
             down_y[y, p] = down_part[y, p]
@@ -446,24 +466,6 @@
             @pl.when(jnp.logical_or(4 * c + k != z, cc != c))
             def _():
                 down_copy(k, cc).start()
-
-        tiles = pl.ds(k * 5, 5)
-        mine = jnp.logical_and(x == k, owns)
-
-        @pl.when(mine)
-        def _():
-            arrived(up_fin.at[0:4], ag_r.at[k])
-
-        @pl.when(jnp.logical_not(mine))
-        def _():
-            arrived(up_fin.at[0:5], ag_r.at[k])
-
-        for d in range(1, NY):
-            yy = (y + d) % NY
-            send(up_fin.at[tiles], up_out.at[c, y, tiles], ay_s.at[0], ay_r.at[k],
-                 at(x, yy, z, c))
-        local(up_fin.at[tiles], up_out.at[c, y, tiles], 18 + k)
-        send(up_fin.at[tiles], up_out.at[c, y, tiles], sh_s.at[0], sh_r.at[0], sibling)
 
     source_core = z // 4
 

time: 67.6 us -> 66.2 us (0.979)
  Pallas kernels: 66.8 us -> 65.4 us
    pallas_call x1, Pallas kernels: 64 us -> 62.6 us  [body(): pl.pallas_call(kernel, out_shape=[shape((1, 128, 4096), BF), shape((1, 12...]
where the time goes in v5:
time: 66.2 us; the launch traced here: 66.1 us
  Pallas kernels  65.4 us (99%)
    pallas_call x1, Pallas kernels, body(): pl.pallas_call(kernel, out_shape=[shape((1, 128, 4096), BF), shape((1, 12...  62.6 us
    pallas_call x1, Pallas kernels, body(): pl.pallas_call(finish, out_shape=[shape((1, 128, 4096), BF), shape((1, 12...  2.82 us

profile of v5, /device:TPU:1, one launch (start us, length us, event | category | flops | bytes accessed | tf_op | source)
XLA Modules:
  0.0 66.1 jit_solution(9662615049254265295)
XLA Ops:
  0.6 62.6 %shard_map.153 = (bf16[1,128,4096]{2,1,0:T(8,128)(2,1)}, bf16[1,128,512]{2,1,0:T(8,128)(2,1)}, bf16[1,128,512]{2,1,0:T(8,128)(2,1)}, f32[32,192]{1,0:T(8,128)}, bf16[2,4,20,16,128]{4,3,2,1,0:T(8,128)(2,1)}) custom-call(bf16[1,128,8192]{2,1,0:T(8,128)(2,1)} %x_in.1, bf16[1,128,4096]{2,1,0:T(8,128)(2,1)} %q_in.1, bf16[1,128,512]{2,1,0:T(8,128)(2,1)} %k_in.1, ...), custom_call_target="tpu_custom_call" | custom-call | flops 8000000000 | bytes 12582912 | tf_op jit(solution)/shard_map/pallas_call | solution.py:619
  63.2 2.8 %shard_map.154 = (bf16[1,128,4096]{2,1,0:T(8,128)(2,1)}, bf16[1,128,512]{2,1,0:T(8,128)(2,1)}, bf16[1,128,512]{2,1,0:T(8,128)(2,1)}, f32[32,192]{1,0:T(8,128)}, ...) custom-call(bf16[1,128,4096]{2,1,0:T(8,128)(2,1)} %get-tuple-element.12.dq_in, ...), custom_call_target="tpu_custom_call" | custom-call | flops 1000000 | bytes 6291456 | tf_op jit(solution)/shard_map/pallas_call | solution.py:635
